TPU v7x, 32 devices: a whole 2x2x4 slice. The times are simulated.
32 devices in a mesh: tm: 8 (over z, y), col: 4 (over x, core).
Axes of the slice: x: 2, y: 2, z: 4, core: 2. Of those that a mesh axis runs over, the one named last changes fastest.
Arguments:
- frames: bfloat16 [24, 2, 96, 384], P('tm', None, 'col'), may hold values from -6 to 6
- up_kernel: bfloat16 [10368, 256], P(None, 'tm'), may hold values from -0.109375 to 0.109375
- mix_kernel: bfloat16 [6912, 256], P(None, 'tm'), may hold values from -0.078125 to 0.078125
- cotangent: bfloat16 [48, 2, 96, 256], P('tm', None, 'col'), may hold values from -6 to 6
Outputs:
- decoded: bfloat16 [48, 2, 96, 256], P('tm', None, 'col')
- frames_grad: bfloat16 [24, 2, 96, 384], P('tm', None, 'col')
All inputs are finite; a program needn't handle non-finite values.
Results may differ from a plain program's by a relative error of at most 0.005.
Values may be sent and summed in bfloat16 or wider, within the bound.
A program may use at most 64 MiB of HBM per device.

v0:
```python
import jax
import jax.numpy as jnp
from jax import lax
from jax.sharding import PartitionSpec as P


def with_halo(block, sides, width):
    for axis, dim in sides:
        count = lax.axis_size(axis)
        forward = [(i, i + 1) for i in range(count - 1)]
        backward = [(target, source) for source, target in forward]
        low = lax.ppermute(
            lax.slice_in_dim(block, block.shape[dim] - width, None, axis=dim), axis, forward
        )
        high = lax.ppermute(lax.slice_in_dim(block, 0, width, axis=dim), axis, backward)
        block = jnp.concatenate([low, block, high], axis=dim)
    return block


def from_behind(array, axis, by):
    devices = lax.axis_size(axis)
    pairs = [(i, i + by) for i in range(devices) if 0 <= i + by < devices]
    return lax.ppermute(array, axis, pairs)


def widen(field):
    return with_halo(field, (("col", 2),), 1)


def from_previous(field):
    return from_behind(field, "tm", 1)


def from_next(field):
    return from_behind(field, "tm", -1)


def forward_pass(kernel, produce):
    return produce(lax.all_gather(kernel, "tm", axis=1, tiled=True), jnp.int32(0))


def backward_pass(kernel, combine, initial):
    return combine(initial, lax.all_gather(kernel, "tm", axis=1, tiled=True), jnp.int32(0))


def pad_rows(field):
    return jnp.pad(field, ((0, 0), (1, 1), (0, 0), (0, 0)))


def window(padded, first, count, row_low, col_low, height, width):
    part = padded[first : first + count, row_low : row_low + height, col_low : col_low + width]
    return part.reshape(-1, part.shape[-1])


def transposed(rows, matrix):
    return lax.dot_general(
        rows, matrix, (((1,), (1,)), ((), ())), preferred_element_type=jnp.float32
    )


def shards(frames, up_kernel, mix_kernel, cotangent):
    frame_count, height, width, in_channels = frames.shape
    out_channels = mix_kernel.shape[0] // 27
    count = 2 * frame_count
    block = count * height * width
    widened = widen(frames)
    earlier = from_previous(widened[-1:])
    extended = pad_rows(jnp.concatenate((earlier, widened), axis=0))
    rows_in = extended.shape[0] - 1

    def up_columns(piece, start):
        taps = piece.reshape(3, 3, 3, in_channels, piece.shape[1])
        even = jnp.zeros((rows_in * height * width, piece.shape[1]), jnp.float32)
        odd = even
        for tap_h in range(3):
            for tap_w in range(3):
                current = window(extended, 1, rows_in, tap_h, tap_w, height, width)
                prior = window(extended, 0, rows_in, tap_h, tap_w, height, width)
                even = even + jnp.dot(
                    current, taps[0, tap_h, tap_w], preferred_element_type=jnp.float32
                )
                even = even + jnp.dot(
                    prior, taps[2, tap_h, tap_w], preferred_element_type=jnp.float32
                )
                odd = odd + jnp.dot(
                    current, taps[1, tap_h, tap_w], preferred_element_type=jnp.float32
                )
        stacked = jnp.stack(
            (even.reshape(rows_in, height * width, -1), odd.reshape(rows_in, height * width, -1)),
            axis=1,
        )
        return stacked.reshape(-1, piece.shape[1])

    before_all = forward_pass(up_kernel, up_columns).reshape(
        2 * rows_in, height, width, out_channels
    )
    hidden = jax.nn.silu(before_all).astype(jnp.bfloat16)
    earlier_hidden = from_previous(hidden[-2:])
    hidden_pad = pad_rows(widen(jnp.concatenate((earlier_hidden, hidden), axis=0)))
    cot_pad = pad_rows(widen(jnp.concatenate((cotangent, from_next(cotangent[:2])), axis=0)))

    def mix_forward(piece, start):
        taps = piece.reshape(3, 3, 3, out_channels, piece.shape[1])
        total = jnp.zeros((block, piece.shape[1]), jnp.float32)
        for tap_t in range(3):
            for tap_h in range(3):
                for tap_w in range(3):
                    total = total + jnp.dot(
                        window(hidden_pad, tap_t, count, tap_h, tap_w, height, width),
                        taps[tap_t, tap_h, tap_w],
                        preferred_element_type=jnp.float32,
                    )
        return total

    def mix_backward(piece):
        taps = piece.reshape(3, 3, 3, out_channels, piece.shape[1])
        total = jnp.zeros((block, out_channels), jnp.float32)
        for tap_t in range(3):
            for tap_h in range(3):
                for tap_w in range(3):
                    total = total + transposed(
                        window(cot_pad, 2 - tap_t, count, 2 - tap_h, 2 - tap_w, height, width),
                        taps[tap_t, tap_h, tap_w],
                    )
        return total

    empty = jnp.zeros((block, out_channels), jnp.float32)
    decoded_flat = forward_pass(mix_kernel, mix_forward)

    def accumulate(total, piece, start):
        return mix_backward(piece)

    hidden_grad = backward_pass(mix_kernel, accumulate, empty)
    flat_before = before_all.reshape(block, out_channels)
    sigma = jax.nn.sigmoid(flat_before)
    before_grad = (hidden_grad * sigma * (1.0 + flat_before * (1.0 - sigma))).astype(jnp.bfloat16)
    before_grad = before_grad.reshape(count, height, width, out_channels)
    grad_pad = pad_rows(widen(jnp.concatenate((before_grad, from_next(before_grad[:1])), axis=0)))
    evens = grad_pad[0::2]
    odds = grad_pad[1::2]

    def up_backward(total, piece, start):
        taps = piece.reshape(3, 3, 3, in_channels, piece.shape[1])
        for tap_h in range(3):
            for tap_w in range(3):
                total = total + transposed(
                    window(evens, 0, frame_count, 2 - tap_h, 2 - tap_w, height, width),
                    taps[0, tap_h, tap_w],
                )
                total = total + transposed(
                    window(odds, 0, frame_count, 2 - tap_h, 2 - tap_w, height, width),
                    taps[1, tap_h, tap_w],
                )
                total = total + transposed(
                    window(evens, 1, frame_count, 2 - tap_h, 2 - tap_w, height, width),
                    taps[2, tap_h, tap_w],
                )
        return total

    grad_start = jnp.zeros((frame_count * height * width, in_channels), jnp.float32)
    grad_total = backward_pass(up_kernel, up_backward, grad_start)
    decoded = decoded_flat.astype(jnp.bfloat16).reshape(count, height, width, out_channels)
    frames_grad = grad_total.astype(jnp.bfloat16).reshape(frame_count, height, width, in_channels)
    return (decoded, frames_grad)


def solution(mesh):
    placed = (P("tm", None, "col", None), P(None, "tm"), P(None, "tm"), P("tm", None, "col", None))
    return jax.shard_map(
        shards,
        mesh=mesh,
        in_specs=placed,
        out_specs=(P("tm", None, "col", None), P("tm", None, "col", None)),
        check_vma=False,
    )
```

profile of v0, /device:TPU:0, one launch (start us, length us, event | category | flops | bytes accessed | tf_op | source)
XLA Modules:
  0.0 233.1 jit_solution(10109288774046163512)
XLA Ops:
  7.2 0.7 all-gather.5.cloned.1.call-update
  7.9 0.7 all-gather.3.cloned.1.call-update
  8.6 0.8 fusion.52
  9.5 1.3 collective-permute-start.1
  10.8 3.0 %collective-permute-start = (bf16[3,2,1,384]{3,2,1,0:T(2,128)(2,1)S(1)}, bf16[3,2,1,384]{3,2,1,0:T(2,128)(2,1)S(1)}, u32[]{:S(2)}, u32[]{:S(2)}) collective-permute-start(bf16[3,2,1,384]{3,2,1,0:T(2,128)(2,1)S(1)} %get-tuple-element.113), channel_id=1, source_target_pairs={{0,1},{1,2},{2,3},{4,5},{5,6},{6,7},{8,9},{9,10},{10,11},{12,13},{... | collective-permute-start | bytes 13832 | tf_op jit(solution)/shard_map/ppermute | solution.py:12
  13.8 0.8 slice.702
  14.6 1.3 collective-permute-start.6
  15.9 0.9 constant_dynamic-update-slice_fusion.1
  16.8 0.8 pad_maximum_fusion.7
  17.6 5.5 %collective-permute-start.2 = (bf16[1,2,26,384]{3,2,1,0:T(8,128)(2,1)S(1)}, bf16[1,2,26,384]{3,2,1,0:T(8,128)(2,1)S(1)}, u32[]{:S(2)}, u32[]{:S(2)}) collective-permute-start(bf16[1,2,26,384]{3,2,1,0:T(8,128)(2,1)S(1)} %pad_maximum_fusion.7), channel_id=1, source_target_pairs={{0,4},{4,8},{8,12},{12,16},{16,20},{20,24},{24,28},{1,5},{5,9},{9,... | collective-permute-start | bytes 119816 | tf_op jit(solution)/shard_map/ppermute | solution.py:23
  23.1 1.8 pad_maximum_fusion.5
  24.9 1.3 collective-permute-done.2
  26.2 1.0 maximum_maximum_fusion.1
  27.2 1.3 collective-permute-start.8
  28.5 3.0 %collective-permute-start.7 = (bf16[8,2,1,256]{3,2,1,0:T(2,128)(2,1)S(1)}, bf16[8,2,1,256]{3,2,1,0:T(2,128)(2,1)S(1)}, u32[]{:S(2)}, u32[]{:S(2)}) collective-permute-start(bf16[8,2,1,256]{3,2,1,0:T(2,128)(2,1)S(1)} %get-tuple-element.86), channel_id=1, source_target_pairs={{0,1},{1,2},{2,3},{4,5},{5,6},{6,7},{8,9},{9,10},{10,11},{12,13},{... | collective-permute-start | bytes 24584 | tf_op jit(solution)/shard_map/ppermute | solution.py:12
  31.5 1.2 pad_slice_fusion
  32.9 1.2 pad_maximum_fusion.2
  34.1 1.5 fusion.45
  35.6 43.5 %all-gather.5.cloned.1.call-done = bf16[6912,256]{0,1:T(8,128)(2,1)} async-done(((bf16[6912,32]{0,1:T(8,128)(2,1)}), bf16[6912,256]{0,1:T(8,128)(2,1)}) %all-gather.5.cloned.1.call-update) | async-done | bytes 3538960 | tf_op jit(solution)/shard_map/all_gather | solution.py:39
  79.1 5.0 %copy.14 = bf16[6912,256]{1,0:T(8,128)(2,1)S(1)} copy(bf16[6912,256]{0,1:T(8,128)(2,1)} %all-gather.5.cloned.1.call-done) | data formatting | bytes 7077888 | tf_op jit(solution)/shard_map/all_gather | solution.py:39
  84.2 1.2 fusion.44
  85.4 1.2 fusion.43
  86.6 1.2 fusion.41
  87.8 1.1 fusion.40
  88.9 1.2 fusion.38
  90.1 1.1 convolution_add_fusion.21
  91.3 1.2 convolution_add_fusion.20
  92.5 1.2 convolution_add_fusion.19
  93.7 0.2 fusion.5
  93.9 0.2 convolution_add_fusion.17
  94.2 0.2 convolution_add_fusion.16
  94.4 0.2 convolution_add_fusion.15
  94.9 0.2 convolution_add_fusion.13
  95.7 0.2 fusion.4
  96.2 0.2 convolution_add_fusion.8
  96.6 0.2 convolution_add_fusion.6
  97.4 0.2 fusion.3
  97.6 0.2 fusion.2
  97.9 0.9 convolution_add_fusion.1
  98.8 68.2 %all-gather.3.cloned.1.call-done = bf16[10368,256]{0,1:T(8,128)(2,1)} async-done(((bf16[10368,32]{0,1:T(8,128)(2,1)}), bf16[10368,256]{0,1:T(8,128)(2,1)}) %all-gather.3.cloned.1.call-update) | async-done | bytes 5308432 | tf_op jit(solution)/shard_map/all_gather | solution.py:39
  167.0 8.0 %copy.11 = bf16[10368,256]{1,0:T(8,128)(2,1)} copy(bf16[10368,256]{0,1:T(8,128)(2,1)} %all-gather.3.cloned.1.call-done) | data formatting | bytes 10616832 | tf_op jit(solution)/shard_map/all_gather | solution.py:39
  175.0 1.3 fusion.30
  176.3 1.7 fusion.27
  178.1 1.2 fusion.32
  179.3 1.2 fusion.31
  180.5 1.2 fusion.29
  181.7 1.2 fusion.28
  182.9 1.2 convolution_add_fusion.78
  184.1 1.2 convolution_add_fusion.93
  185.3 1.2 convolution_add_fusion.92
  186.5 1.2 convolution_add_fusion.77
  187.7 1.2 convolution_add_fusion.91
  192.5 0.2 fusion.8
  192.7 1.3 collective-permute-start.9
  194.0 4.4 %collective-permute-done.9 = bf16[1,2,24,256]{3,2,1,0:T(8,128)(2,1)S(1)} collective-permute-done((bf16[1,2,24,256]{3,2,1,0:T(8,128)(2,1)S(1)}, bf16[1,2,24,256]{3,2,1,0:T(8,128)(2,1)S(1)}, u32[]{:S(2)}, u32[]{:S(2)}) %collective-permute-start.9) | collective-permute-done | bytes 24608 | tf_op jit(solution)/shard_map/ppermute | solution.py:23
  198.5 1.3 collective-permute-start.11
  199.8 3.0 %collective-permute-start.10 = (bf16[7,2,1,256]{3,2,1,0:T(2,128)(2,1)S(1)}, bf16[7,2,1,256]{3,2,1,0:T(2,128)(2,1)S(1)}, u32[]{:S(2)}, u32[]{:S(2)}) collective-permute-start(bf16[7,2,1,256]{3,2,1,0:T(2,128)(2,1)S(1)} %get-tuple-element.109), channel_id=1, source_target_pairs={{0,1},{1,2},{2,3},{4,5},{5,6},{6,7},{8,9},{9,10},{10,11},{12,13},{... | collective-permute-start | bytes 21512 | tf_op jit(solution)/shard_map/ppermute | solution.py:12
  202.9 3.4 %collective-permute-start.3 = (bf16[2,2,24,256]{3,2,1,0:T(8,128)(2,1)S(1)}, bf16[2,2,24,256]{3,2,1,0:T(8,128)(2,1)S(1)}, u32[]{:S(2)}, u32[]{:S(2)}) collective-permute-start(bf16[2,2,24,256]{3,2,1,0:T(8,128)(2,1)S(1)} %slice.794), channel_id=1, source_target_pairs={{0,4},{4,8},{8,12},{12,16},{16,20},{20,24},{24,28},{1,5},{5,9},{9,... | collective-permute-start | bytes 147464 | tf_op jit(solution)/shard_map/ppermute | solution.py:23
  212.6 0.9 fusion.9
  213.5 2.7 %collective-permute-start.4 = (bf16[8,2,1,256]{3,2,1,0:T(2,128)(2,1)S(1)}, bf16[8,2,1,256]{3,2,1,0:T(2,128)(2,1)S(1)}, u32[]{:S(2)}, u32[]{:S(2)}) collective-permute-start(bf16[8,2,1,256]{3,2,1,0:T(2,128)(2,1)S(1)} %get-tuple-element.92), channel_id=1, source_target_pairs={{0,1},{1,2},{2,3},{4,5},{5,6},{6,7},{8,9},{9,10},{10,11},{12,13},{... | collective-permute-start | bytes 24584 | tf_op jit(solution)/shard_map/ppermute | solution.py:12
  216.2 1.5 collective-permute-start.5
  217.7 1.8 collective-permute-done.5
  220.1 0.3 fusion.46
  225.4 0.9 fusion.7
  (171 shorter events, 16.9 us)
Async XLA Ops:
  7.2 72.0 %all-gather.5.cloned.1.call-start = ((), (), s32[]{:S(2)}) async-start(), calls=%async_computation.1 | async-start | bytes 3981312 | tf_op jit(solution)/shard_map/all_gather | solution.py:39
  7.9 159.1 %all-gather.3.cloned.1.call-start = ((), (), s32[]{:S(2)}) async-start(), calls=%async_computation | async-start | bytes 5971968 | tf_op jit(solution)/shard_map/all_gather | solution.py:39
  9.5 7.4 %collective-permute-start.1 = (bf16[3,2,1,384]{3,2,1,0:T(2,128)(2,1)S(1)}, bf16[3,2,1,384]{3,2,1,0:T(2,128)(2,1)S(1)}, u32[]{:S(2)}, u32[]{:S(2)}) collective-permute-start(bf16[3,2,1,384]{3,2,1,0:T(2,128)(2,1)S(1)} %get-tuple-element.114), channel_id=1, source_target_pairs={{1,0},{2,1},{3,2},{5,4},{6,5},{7,6},{9,8},{10,9},{11,10},{13,12},{... | collective-permute-start | bytes 13832 | tf_op jit(solution)/shard_map/ppermute | solution.py:15
  10.8 6.1 %collective-permute-start = (bf16[3,2,1,384]{3,2,1,0:T(2,128)(2,1)S(1)}, bf16[3,2,1,384]{3,2,1,0:T(2,128)(2,1)S(1)}, u32[]{:S(2)}, u32[]{:S(2)}) collective-permute-start(bf16[3,2,1,384]{3,2,1,0:T(2,128)(2,1)S(1)} %get-tuple-element.113), channel_id=1, source_target_pairs={{0,1},{1,2},{2,3},{4,5},{5,6},{6,7},{8,9},{9,10},{10,11},{12,13},{... | collective-permute-start | bytes 13832 | tf_op jit(solution)/shard_map/ppermute | solution.py:12
  14.6 12.5 %collective-permute-start.6 = (bf16[2,2,24,256]{3,2,1,0:T(8,128)(2,1)S(1)}, bf16[2,2,24,256]{3,2,1,0:T(8,128)(2,1)S(1)}, u32[]{:S(2)}, u32[]{:S(2)}) collective-permute-start(bf16[2,2,24,256]{3,2,1,0:T(8,128)(2,1)S(1)} %slice.702), channel_id=1, source_target_pairs={{4,0},{8,4},{12,8},{16,12},{20,16},{24,20},{28,24},{5,1},{9,5},{13... | collective-permute-start | bytes 147464 | tf_op jit(solution)/shard_map/ppermute | solution.py:23
  17.6 8.5 %collective-permute-start.2 = (bf16[1,2,26,384]{3,2,1,0:T(8,128)(2,1)S(1)}, bf16[1,2,26,384]{3,2,1,0:T(8,128)(2,1)S(1)}, u32[]{:S(2)}, u32[]{:S(2)}) collective-permute-start(bf16[1,2,26,384]{3,2,1,0:T(8,128)(2,1)S(1)} %pad_maximum_fusion.7), channel_id=1, source_target_pairs={{0,4},{4,8},{8,12},{12,16},{16,20},{20,24},{24,28},{1,5},{5,9},{9,... | collective-permute-start | bytes 119816 | tf_op jit(solution)/shard_map/ppermute | solution.py:23
  27.2 5.6 %collective-permute-start.8 = (bf16[8,2,1,256]{3,2,1,0:T(2,128)(2,1)S(1)}, bf16[8,2,1,256]{3,2,1,0:T(2,128)(2,1)S(1)}, u32[]{:S(2)}, u32[]{:S(2)}) collective-permute-start(bf16[8,2,1,256]{3,2,1,0:T(2,128)(2,1)S(1)} %get-tuple-element.87), channel_id=1, source_target_pairs={{1,0},{2,1},{3,2},{5,4},{6,5},{7,6},{9,8},{10,9},{11,10},{13,12},{... | collective-permute-start | bytes 24584 | tf_op jit(solution)/shard_map/ppermute | solution.py:15
  28.5 4.3 %collective-permute-start.7 = (bf16[8,2,1,256]{3,2,1,0:T(2,128)(2,1)S(1)}, bf16[8,2,1,256]{3,2,1,0:T(2,128)(2,1)S(1)}, u32[]{:S(2)}, u32[]{:S(2)}) collective-permute-start(bf16[8,2,1,256]{3,2,1,0:T(2,128)(2,1)S(1)} %get-tuple-element.86), channel_id=1, source_target_pairs={{0,1},{1,2},{2,3},{4,5},{5,6},{6,7},{8,9},{9,10},{10,11},{12,13},{... | collective-permute-start | bytes 24584 | tf_op jit(solution)/shard_map/ppermute | solution.py:12
  84.1 9.5 %copy-start.12 = (bf16[6,2,24,256]{3,2,1,0:T(8,128)(2,1)S(1)}, bf16[6,2,24,256]{3,2,1,0:T(8,128)(2,1)}, u32[]{:S(2)}) copy-start(bf16[6,2,24,256]{3,2,1,0:T(8,128)(2,1)} %get-tuple-element.85) | copy-start | bytes 442372
  84.1 9.8 %copy-start.27 = (bf16[6,2,24,256]{3,2,1,0:T(8,128)(2,1)S(1)}, bf16[6,2,24,256]{3,2,1,0:T(8,128)(2,1)}, u32[]{:S(2)}) copy-start(bf16[6,2,24,256]{3,2,1,0:T(8,128)(2,1)} %get-tuple-element.16) | copy-start | bytes 442372
  84.1 10.0 %copy-start.26 = (bf16[6,2,24,256]{3,2,1,0:T(8,128)(2,1)S(1)}, bf16[6,2,24,256]{3,2,1,0:T(8,128)(2,1)}, u32[]{:S(2)}) copy-start(bf16[6,2,24,256]{3,2,1,0:T(8,128)(2,1)} %get-tuple-element.15) | copy-start | bytes 442372
  84.1 10.3 %copy-start.25 = (bf16[6,2,24,256]{3,2,1,0:T(8,128)(2,1)S(1)}, bf16[6,2,24,256]{3,2,1,0:T(8,128)(2,1)}, u32[]{:S(2)}) copy-start(bf16[6,2,24,256]{3,2,1,0:T(8,128)(2,1)} %get-tuple-element.14) | copy-start | bytes 442372
  84.2 10.5 %copy-start.24 = (bf16[6,2,24,256]{3,2,1,0:T(8,128)(2,1)S(1)}, bf16[6,2,24,256]{3,2,1,0:T(8,128)(2,1)}, u32[]{:S(2)}) copy-start(bf16[6,2,24,256]{3,2,1,0:T(8,128)(2,1)} %get-tuple-element.13) | copy-start | bytes 442372
  84.2 10.8 %copy-start.23 = (bf16[6,2,24,256]{3,2,1,0:T(8,128)(2,1)S(1)}, bf16[6,2,24,256]{3,2,1,0:T(8,128)(2,1)}, u32[]{:S(2)}) copy-start(bf16[6,2,24,256]{3,2,1,0:T(8,128)(2,1)} %get-tuple-element.12) | copy-start | bytes 442372
  85.4 9.8 %copy-start.22 = (bf16[6,2,24,256]{3,2,1,0:T(8,128)(2,1)S(1)}, bf16[6,2,24,256]{3,2,1,0:T(8,128)(2,1)}, u32[]{:S(2)}) copy-start(bf16[6,2,24,256]{3,2,1,0:T(8,128)(2,1)} %get-tuple-element.11) | copy-start | bytes 442372
  86.6 8.8 %copy-start.13 = (bf16[6,2,24,256]{3,2,1,0:T(8,128)(2,1)S(1)}, bf16[6,2,24,256]{3,2,1,0:T(8,128)(2,1)}, u32[]{:S(2)}) copy-start(bf16[6,2,24,256]{3,2,1,0:T(8,128)(2,1)} %get-tuple-element.81) | copy-start | bytes 442372
  88.9 6.7 %copy-start.11 = (bf16[6,2,24,256]{3,2,1,0:T(8,128)(2,1)S(1)}, bf16[6,2,24,256]{3,2,1,0:T(8,128)(2,1)}, u32[]{:S(2)}) copy-start(bf16[6,2,24,256]{3,2,1,0:T(8,128)(2,1)} %get-tuple-element.84) | copy-start | bytes 442372
  91.3 4.6 %copy-start.21 = (bf16[6,2,24,256]{3,2,1,0:T(8,128)(2,1)S(1)}, bf16[6,2,24,256]{3,2,1,0:T(8,128)(2,1)}, u32[]{:S(2)}) copy-start(bf16[6,2,24,256]{3,2,1,0:T(8,128)(2,1)} %get-tuple-element.10) | copy-start | bytes 442372
  92.5 3.7 %copy-start.20 = (bf16[6,2,24,256]{3,2,1,0:T(8,128)(2,1)S(1)}, bf16[6,2,24,256]{3,2,1,0:T(8,128)(2,1)}, u32[]{:S(2)}) copy-start(bf16[6,2,24,256]{3,2,1,0:T(8,128)(2,1)} %get-tuple-element.9) | copy-start | bytes 442372
  93.6 2.8 %copy-start.19 = (bf16[6,2,24,256]{3,2,1,0:T(8,128)(2,1)S(1)}, bf16[6,2,24,256]{3,2,1,0:T(8,128)(2,1)}, u32[]{:S(2)}) copy-start(bf16[6,2,24,256]{3,2,1,0:T(8,128)(2,1)} %get-tuple-element.8) | copy-start | bytes 442372
  93.7 3.0 %copy-start.18 = (bf16[6,2,24,256]{3,2,1,0:T(8,128)(2,1)S(1)}, bf16[6,2,24,256]{3,2,1,0:T(8,128)(2,1)}, u32[]{:S(2)}) copy-start(bf16[6,2,24,256]{3,2,1,0:T(8,128)(2,1)} %get-tuple-element.7) | copy-start | bytes 442372
  93.9 3.0 %copy-start.17 = (bf16[6,2,24,256]{3,2,1,0:T(8,128)(2,1)S(1)}, bf16[6,2,24,256]{3,2,1,0:T(8,128)(2,1)}, u32[]{:S(2)}) copy-start(bf16[6,2,24,256]{3,2,1,0:T(8,128)(2,1)} %get-tuple-element.6) | copy-start | bytes 442372
  94.2 3.0 %copy-start.16 = (bf16[6,2,24,256]{3,2,1,0:T(8,128)(2,1)S(1)}, bf16[6,2,24,256]{3,2,1,0:T(8,128)(2,1)}, u32[]{:S(2)}) copy-start(bf16[6,2,24,256]{3,2,1,0:T(8,128)(2,1)} %get-tuple-element.5) | copy-start | bytes 442372
  94.4 2.9 %copy-start.10 = (bf16[6,2,24,256]{3,2,1,0:T(8,128)(2,1)S(1)}, bf16[6,2,24,256]{3,2,1,0:T(8,128)(2,1)}, u32[]{:S(2)}) copy-start(bf16[6,2,24,256]{3,2,1,0:T(8,128)(2,1)} %get-tuple-element.83) | copy-start | bytes 442372
  94.9 2.7 %copy-start.9 = (bf16[6,2,24,256]{3,2,1,0:T(8,128)(2,1)S(1)}, bf16[6,2,24,256]{3,2,1,0:T(8,128)(2,1)}, u32[]{:S(2)}) copy-start(bf16[6,2,24,256]{3,2,1,0:T(8,128)(2,1)} %get-tuple-element.66) | copy-start | bytes 442372
  95.2 2.7 %copy-start.15 = (bf16[6,2,24,256]{3,2,1,0:T(8,128)(2,1)S(1)}, bf16[6,2,24,256]{3,2,1,0:T(8,128)(2,1)}, u32[]{:S(2)}) copy-start(bf16[6,2,24,256]{3,2,1,0:T(8,128)(2,1)} %get-tuple-element.3) | copy-start | bytes 442372
  175.0 13.9 %copy-start = (bf16[10368,256]{1,0:T(8,128)(2,1)S(1)}, bf16[10368,256]{1,0:T(8,128)(2,1)}, u32[]{:S(2)}) copy-start(bf16[10368,256]{1,0:T(8,128)(2,1)} %copy.11) | copy-start | bytes 15925252
  175.0 13.9 %copy-start.6 = (bf16[3,2,24,384]{3,2,1,0:T(8,128)(2,1)S(1)}, bf16[3,2,24,384]{3,2,1,0:T(8,128)(2,1)}, u32[]{:S(2)}) copy-start(bf16[3,2,24,384]{3,2,1,0:T(8,128)(2,1)} %get-tuple-element.98) | copy-start | bytes 331780
  175.0 14.1 %copy-start.32 = (bf16[3,2,24,384]{3,2,1,0:T(8,128)(2,1)S(1)}, bf16[3,2,24,384]{3,2,1,0:T(8,128)(2,1)}, u32[]{:S(2)}) copy-start(bf16[3,2,24,384]{3,2,1,0:T(8,128)(2,1)} %get-tuple-element.99) | copy-start | bytes 331780
  175.0 14.3 %copy-start.8 = (bf16[3,2,24,384]{3,2,1,0:T(8,128)(2,1)S(1)}, bf16[3,2,24,384]{3,2,1,0:T(8,128)(2,1)}, u32[]{:S(2)}) copy-start(bf16[3,2,24,384]{3,2,1,0:T(8,128)(2,1)} %get-tuple-element.112) | copy-start | bytes 331780
  175.0 14.6 %copy-start.1 = (bf16[3,2,24,384]{3,2,1,0:T(8,128)(2,1)S(1)}, bf16[3,2,24,384]{3,2,1,0:T(8,128)(2,1)}, u32[]{:S(2)}) copy-start(bf16[3,2,24,384]{3,2,1,0:T(8,128)(2,1)} %param.4) | copy-start | bytes 331780
  175.0 14.8 %copy-start.31 = (bf16[3,2,24,384]{3,2,1,0:T(8,128)(2,1)S(1)}, bf16[3,2,24,384]{3,2,1,0:T(8,128)(2,1)}, u32[]{:S(2)}) copy-start(bf16[3,2,24,384]{3,2,1,0:T(8,128)(2,1)} %get-tuple-element.106) | copy-start | bytes 331780
  175.0 15.0 %copy-start.7 = (bf16[3,2,24,384]{3,2,1,0:T(8,128)(2,1)S(1)}, bf16[3,2,24,384]{3,2,1,0:T(8,128)(2,1)}, u32[]{:S(2)}) copy-start(bf16[3,2,24,384]{3,2,1,0:T(8,128)(2,1)} %get-tuple-element.111) | copy-start | bytes 331780
  175.0 15.2 %copy-start.3 = (bf16[3,2,24,384]{3,2,1,0:T(8,128)(2,1)S(1)}, bf16[3,2,24,384]{3,2,1,0:T(8,128)(2,1)}, u32[]{:S(2)}) copy-start(bf16[3,2,24,384]{3,2,1,0:T(8,128)(2,1)} %get-tuple-element.100) | copy-start | bytes 331780
  179.3 11.5 %copy-start.5 = (bf16[3,2,24,384]{3,2,1,0:T(8,128)(2,1)S(1)}, bf16[3,2,24,384]{3,2,1,0:T(8,128)(2,1)}, u32[]{:S(2)}) copy-start(bf16[3,2,24,384]{3,2,1,0:T(8,128)(2,1)} %get-tuple-element.102) | copy-start | bytes 331780
  180.5 10.5 %copy-start.30 = (bf16[3,2,24,384]{3,2,1,0:T(8,128)(2,1)S(1)}, bf16[3,2,24,384]{3,2,1,0:T(8,128)(2,1)}, u32[]{:S(2)}) copy-start(bf16[3,2,24,384]{3,2,1,0:T(8,128)(2,1)} %get-tuple-element.101) | copy-start | bytes 331780
  182.9 8.5 %copy-start.4 = (bf16[3,2,24,384]{3,2,1,0:T(8,128)(2,1)S(1)}, bf16[3,2,24,384]{3,2,1,0:T(8,128)(2,1)}, u32[]{:S(2)}) copy-start(bf16[3,2,24,384]{3,2,1,0:T(8,128)(2,1)} %get-tuple-element.104) | copy-start | bytes 331780
  184.1 7.5 %copy-start.29 = (bf16[3,2,24,384]{3,2,1,0:T(8,128)(2,1)S(1)}, bf16[3,2,24,384]{3,2,1,0:T(8,128)(2,1)}, u32[]{:S(2)}) copy-start(bf16[3,2,24,384]{3,2,1,0:T(8,128)(2,1)} %get-tuple-element.103) | copy-start | bytes 331780
  186.5 5.5 %copy-start.28 = (bf16[3,2,24,384]{3,2,1,0:T(8,128)(2,1)S(1)}, bf16[3,2,24,384]{3,2,1,0:T(8,128)(2,1)}, u32[]{:S(2)}) copy-start(bf16[3,2,24,384]{3,2,1,0:T(8,128)(2,1)} %get-tuple-element.94) | copy-start | bytes 331780
  189.3 3.1 %copy-start.2 = (f32[288,256]{1,0:T(8,128)S(1)}, f32[288,256]{1,0:T(8,128)}, u32[]{:S(2)}) copy-start(f32[288,256]{1,0:T(8,128)} %convolution_add_fusion.1) | copy-start | bytes 884740
  189.3 3.1 %copy-start.14 = (bf16[6,2,24,256]{3,2,1,0:T(8,128)(2,1)S(1)}, bf16[6,2,24,256]{3,2,1,0:T(8,128)(2,1)}, u32[]{:S(2)}) copy-start(bf16[6,2,24,256]{3,2,1,0:T(8,128)(2,1)} %get-tuple-element.2) | copy-start | bytes 442372
  192.7 5.7 %collective-permute-start.9 = (bf16[1,2,24,256]{3,2,1,0:T(8,128)(2,1)S(1)}, bf16[1,2,24,256]{3,2,1,0:T(8,128)(2,1)S(1)}, u32[]{:S(2)}, u32[]{:S(2)}) collective-permute-start(bf16[1,2,24,256]{3,2,1,0:T(8,128)(2,1)S(1)} %bitcast.672), channel_id=1, source_target_pairs={{4,0},{8,4},{12,8},{16,12},{20,16},{24,20},{28,24},{5,1},{9,5},{13... | collective-permute-start | bytes 73736 | tf_op jit(solution)/shard_map/ppermute | solution.py:23
  198.5 7.8 %collective-permute-start.11 = (bf16[7,2,1,256]{3,2,1,0:T(2,128)(2,1)S(1)}, bf16[7,2,1,256]{3,2,1,0:T(2,128)(2,1)S(1)}, u32[]{:S(2)}, u32[]{:S(2)}) collective-permute-start(bf16[7,2,1,256]{3,2,1,0:T(2,128)(2,1)S(1)} %get-tuple-element.110), channel_id=1, source_target_pairs={{1,0},{2,1},{3,2},{5,4},{6,5},{7,6},{9,8},{10,9},{11,10},{13,12},{... | collective-permute-start | bytes 21512 | tf_op jit(solution)/shard_map/ppermute | solution.py:15
  199.8 6.5 %collective-permute-start.10 = (bf16[7,2,1,256]{3,2,1,0:T(2,128)(2,1)S(1)}, bf16[7,2,1,256]{3,2,1,0:T(2,128)(2,1)S(1)}, u32[]{:S(2)}, u32[]{:S(2)}) collective-permute-start(bf16[7,2,1,256]{3,2,1,0:T(2,128)(2,1)S(1)} %get-tuple-element.109), channel_id=1, source_target_pairs={{0,1},{1,2},{2,3},{4,5},{5,6},{6,7},{8,9},{9,10},{10,11},{12,13},{... | collective-permute-start | bytes 21512 | tf_op jit(solution)/shard_map/ppermute | solution.py:12
  202.9 10.5 %collective-permute-start.3 = (bf16[2,2,24,256]{3,2,1,0:T(8,128)(2,1)S(1)}, bf16[2,2,24,256]{3,2,1,0:T(8,128)(2,1)S(1)}, u32[]{:S(2)}, u32[]{:S(2)}) collective-permute-start(bf16[2,2,24,256]{3,2,1,0:T(8,128)(2,1)S(1)} %slice.794), channel_id=1, source_target_pairs={{0,4},{4,8},{8,12},{12,16},{16,20},{20,24},{24,28},{1,5},{5,9},{9,... | collective-permute-start | bytes 147464 | tf_op jit(solution)/shard_map/ppermute | solution.py:23
  213.5 4.2 %collective-permute-start.4 = (bf16[8,2,1,256]{3,2,1,0:T(2,128)(2,1)S(1)}, bf16[8,2,1,256]{3,2,1,0:T(2,128)(2,1)S(1)}, u32[]{:S(2)}, u32[]{:S(2)}) collective-permute-start(bf16[8,2,1,256]{3,2,1,0:T(2,128)(2,1)S(1)} %get-tuple-element.92), channel_id=1, source_target_pairs={{0,1},{1,2},{2,3},{4,5},{5,6},{6,7},{8,9},{9,10},{10,11},{12,13},{... | collective-permute-start | bytes 24584 | tf_op jit(solution)/shard_map/ppermute | solution.py:12
  216.2 3.4 %collective-permute-start.5 = (bf16[8,2,1,256]{3,2,1,0:T(2,128)(2,1)S(1)}, bf16[8,2,1,256]{3,2,1,0:T(2,128)(2,1)S(1)}, u32[]{:S(2)}, u32[]{:S(2)}) collective-permute-start(bf16[8,2,1,256]{3,2,1,0:T(2,128)(2,1)S(1)} %get-tuple-element.93), channel_id=1, source_target_pairs={{1,0},{2,1},{3,2},{5,4},{6,5},{7,6},{9,8},{10,9},{11,10},{13,12},{... | collective-permute-start | bytes 24584 | tf_op jit(solution)/shard_map/ppermute | solution.py:15
Sparse Core Ops, SparseCore 0:
  10.2 68.9 all-gather.4
  81.3 85.6 all-gather.2
where the time goes:
time: 236 us; the launch traced here: 233 us
  waiting for transfers between devices  121 us (51%)
  matrix products  43.7 us (19%)
  starting transfers between devices  28.7 us (12%)
  local copies, waits for them, and re-layouts  19.1 us (8%)
  between operations  15.6 us (7%)
  other arithmetic  5.54 us (2%)
    all_gather x2, waiting for transfers between devices, forward_pass(): lax.all_gather(kernel, 'tm', axis=1, tiled=True)  112 us
    dot_general x54, matrix products, transposed(): lax.dot_general(rows, matrix, (((1,), (1,)), ((), ())), preferred_element...  21 us
    all_gather x2, local copies, waits for them, and re-layouts, forward_pass(): lax.all_gather(kernel, 'tm', axis=1, tiled=True)  12.9 us
    ppermute x4, starting transfers between devices, with_halo(): lax.ppermute(lax.slice_in_dim(block, block.shape[dim] - width, None, axis...  11.8 us
    ppermute x4, starting transfers between devices, from_behind(): return lax.ppermute(array, axis, pairs)  11.4 us
    dot_general x9, matrix products, up_columns(): jnp.dot(current, taps[1, tap_h, tap_w], preferred_element_type=jnp.float32)  6.87 us
    dot_general x27, matrix products, mix_forward(): jnp.dot(window(hidden_pad, tap_t, count, tap_h, tap_w, height, width), ta...  5.87 us
    dot_general x9, matrix products, up_columns(): jnp.dot(prior, taps[2, tap_h, tap_w], preferred_element_type=jnp.float32)  5.7 us
  transfers between devices with their start and end apart: 14, of which 5 were waited for; matrix products, arithmetic and copies ran while one was open for 16% of the time, Pallas kernels for 0%

commit v1 on v0

--- a/solution.py
+++ b/solution.py
@@ -1,6 +1,10 @@
+import functools
+
 import jax
 import jax.numpy as jnp
 from jax import lax
+from jax.experimental import pallas as pl
+from jax.experimental.pallas import tpu as pltpu
 from jax.sharding import PartitionSpec as P
 
 
@@ -164,10 +168,411 @@
     return (decoded, frames_grad)
 
 
+MESH_ID = pl.DeviceIdType.MESH
+BF16 = jnp.bfloat16
+F32 = jnp.float32
+
+
+def shifted(rows, by):
+    if by == 0:
+        return rows
+    count = rows.shape[0]
+    place = lax.broadcasted_iota(jnp.int32, rows.shape, 0)
+    if by < 0:
+        return jnp.where(place == 0, 0.0, pltpu.roll(rows, 1, 0))
+    return jnp.where(place == count - 1, 0.0, pltpu.roll(rows, count - 1, 0))
+
+
+def pairs(parts):
+    if len(parts) % 2:
+        parts = parts + [jnp.zeros_like(parts[0])]
+    return [
+        jnp.concatenate((parts[i], parts[i + 1]), axis=1).astype(BF16)
+        for i in range(0, len(parts), 2)
+    ]
+
+
+def ring_tm(place, n):
+    half = place // (n // 2)
+    level = place + half * (n - 1 - 2 * place)
+    return 2 * level + half
+
+
+def fused_kernel(
+    n, up_ref, mix_ref, frames_ref, cot_ref, decoded_ref, grad_ref,
+    up_all, mix_all, frames_all, cot_all, up_taps, inputs, raw, before, hidden, patches,
+    cots, spread, grads, part_d, part_g, got_d, got_g, sum_d, sum_g, last_d, last_g,
+    ring_send, ring_recv, halo_send, halo_recv, col_send, col_recv, out_send, out_recv,
+):
+    me, q = lax.axis_index("tm"), lax.axis_index("col")
+    sibling = q + 1 - 2 * (q % 2)
+    across = (q + 2) % 4
+    diagonal = (sibling + 2) % 4
+    level, side = me // 2, me % 2
+    place = level + side * (n - 1 - 2 * level)
+    right, left = ring_tm((place + 1) % n, n), ring_tm((place + n - 1) % n, n)
+    after, ahead = (me + 1) % n, (me + n - 1) % n
+    count, in_channels = frames_ref.shape[0], frames_ref.shape[3]
+    times, channels = cot_ref.shape[0], cot_ref.shape[3]
+    cols = frames_ref.shape[2]
+    width = 4 * cols
+    small = channels // 4
+    rows = mix_ref.shape[0]
+    span = 9 * small + small
+
+    def remote(src, dst, send, recv, tm, col):
+        return pltpu.make_async_remote_copy(
+            src_ref=src, dst_ref=dst, send_sem=send, recv_sem=recv,
+            device_id=(tm, col), device_id_type=MESH_ID,
+        )
+
+    barrier = pltpu.get_barrier_semaphore()
+    for tm, col in ((left, q), (right, q), (after, q), (ahead, q), (me, sibling), (me, across)):
+        pl.semaphore_signal(barrier, inc=1, device_id=(tm, col), device_id_type=MESH_ID)
+
+    source = lax.broadcasted_iota(jnp.int32, (channels, 2 * small), 0)
+    lane = lax.broadcasted_iota(jnp.int32, (channels, 2 * small), 1)
+    lane_low = lane % small
+    wanted = rows * (lane_low // 8) + 8 * q + lane_low % 8
+    first = jnp.where((source == wanted) & (lane < small), 1.0, 0.0).astype(BF16)
+    second = jnp.where((source == wanted) & (lane >= small), 1.0, 0.0).astype(BF16)
+    mine = pl.ds(pl.multiple_of(me * rows, rows), rows)
+    for tap_h in range(3):
+        order = [(kt * 3 + tap_h) * 3 + kw for kw in range(3) for kt in range(3)]
+        for i in range(0, 10, 2):
+            picked = jnp.dot(
+                mix_ref[:, order[i] * channels : (order[i] + 1) * channels], first,
+                preferred_element_type=F32,
+            )
+            if i < 8:
+                picked = picked + jnp.dot(
+                    mix_ref[:, order[i + 1] * channels : (order[i + 1] + 1) * channels], second,
+                    preferred_element_type=F32,
+                )
+            start = tap_h * span + i * small
+            mix_all[mine, start : start + 2 * small] = picked.astype(BF16)
+    up_all[me] = up_ref[...]
+    frames_all[q, 2 : 2 + count] = frames_ref[...]
+    cot_all[q, 0:times] = cot_ref[...]
+    pl.semaphore_wait(barrier, 6)
+
+    def ring(direction, kind, step):
+        owner = ring_tm((place + (n - step if direction == 0 else step)) % n, n)
+        target = right if direction == 0 else left
+        ref = up_all.at[owner] if kind == 0 else mix_all.at[
+            pl.ds(pl.multiple_of(owner * rows, rows), rows)
+        ]
+        return remote(
+            ref, ref, ring_send.at[direction, kind, step], ring_recv.at[direction, kind, step],
+            target, q,
+        )
+
+    def steps_of(direction, kind):
+        return n // 2 if direction == kind else n // 2 - 1
+
+    copies = {}
+
+    def ring_start(kind, step):
+        for direction in range(2):
+            if step < steps_of(direction, kind):
+                copies[direction, kind, step] = ring(direction, kind, step)
+                copies[direction, kind, step].start()
+
+    def ring_got(kind, step):
+        for direction in range(2):
+            if step < steps_of(direction, kind):
+                copies[direction, kind, step].wait_recv()
+
+    ring_start(0, 0)
+    halos = [
+        remote(frames_ref.at[count - 2 : count], frames_all.at[q, 0:2],
+               halo_send.at[0], halo_recv.at[0], after, q),
+        remote(frames_ref.at[0:1], frames_all.at[q, count + 2 : count + 3],
+               halo_send.at[1], halo_recv.at[1], ahead, q),
+        remote(cot_ref.at[0:3], cot_all.at[q, times : times + 3],
+               halo_send.at[2], halo_recv.at[2], ahead, q),
+    ]
+    for copy in halos:
+        copy.start()
+    ring_start(1, 0)
+    for copy in halos:
+        copy.wait_recv()
+
+    @pl.when(me == 0)
+    def _():
+        frames_all[q, 0:2] = jnp.zeros((2,) + frames_ref.shape[1:], BF16)
+
+    @pl.when(me == n - 1)
+    def _():
+        frames_all[q, count + 2 : count + 3] = jnp.zeros((1,) + frames_ref.shape[1:], BF16)
+        cot_all[q, times : times + 3] = jnp.zeros((3,) + cot_ref.shape[1:], BF16)
+
+    crossing = [
+        remote(ref.at[q], ref.at[q], col_send.at[i], col_recv.at[i], me, across)
+        for i, ref in enumerate((frames_all, cot_all))
+    ]
+    beside = [
+        remote(ref.at[q], ref.at[q], col_send.at[2 + i], col_recv.at[2 + i], me, sibling)
+        for i, ref in enumerate((frames_all, cot_all))
+    ]
+    for copy in crossing + beside:
+        copy.start()
+    ring_got(0, 0)
+    ring_start(0, 1)
+    ring_got(1, 0)
+    ring_start(1, 1)
+    for copy in crossing:
+        copy.wait_recv()
+    passed = [
+        remote(ref.at[across], ref.at[across], col_send.at[4 + i], col_recv.at[4 + i], me, sibling)
+        for i, ref in enumerate((frames_all, cot_all))
+    ]
+    for copy in passed:
+        copy.start()
+    ring_got(0, 1)
+    ring_start(0, 2)
+    ring_got(1, 1)
+    ring_start(1, 2)
+    for copy in beside + passed:
+        copy.wait_recv()
+
+    @pl.loop(0, count + 3)
+    def _(t):
+        for r in range(2):
+            line = jnp.concatenate([frames_all[c, t, r].astype(F32) for c in range(4)], axis=0)
+            at = pl.ds(pl.multiple_of(t * width, width), width)
+            for kw in range(3):
+                inputs[r, at, kw * in_channels : (kw + 1) * in_channels] = shifted(
+                    line, kw - 1
+                ).astype(BF16)
+
+    @pl.loop(0, times + 3)
+    def _(t):
+        for r in range(2):
+            line = jnp.concatenate([cot_all[c, t, r].astype(F32) for c in range(4)], axis=0)
+            cots[r, pl.ds(pl.multiple_of(t * width, width), width)] = line.astype(BF16)
+
+    ring_got(0, 2)
+    ring_start(0, 3)
+    ring_got(1, 2)
+    ring_start(1, 3)
+    ring_got(0, 3)
+
+    taken = 9 * in_channels
+    for kt in range(3):
+        for start in range(0, taken, in_channels):
+            part = up_all[:, kt * 8 : kt * 8 + 8, start : start + in_channels].astype(F32)
+            up_taps[kt * small : (kt + 1) * small, start : start + in_channels] = part.reshape(
+                small, in_channels
+            ).astype(BF16)
+    up_taps[3 * small : 4 * small] = jnp.zeros((small, taken), BF16)
+
+    wide = 3 * in_channels
+    for r in range(2):
+        total = None
+        for r_in in range(2):
+            kh = r_in - r + 1
+            term = lax.dot_general(
+                inputs[r_in], up_taps[:, kh * wide : (kh + 1) * wide],
+                (((1,), (1,)), ((), ())), preferred_element_type=F32,
+            )
+            total = term if total is None else total + term
+        raw[r] = total
+
+    def frame(t):
+        return slice(t * width, (t + 1) * width)
+
+    for r in range(2):
+        for t in range(times + 3):
+            if t % 2 == 0:
+                value = raw[r, frame(t // 2 + 1), 0:small] + raw[
+                    r, frame(t // 2), 2 * small : 3 * small
+                ]
+            else:
+                value = raw[r, frame((t + 1) // 2), small : 2 * small]
+            before[r, frame(t)] = value
+            active = value / (1.0 + jnp.exp(-value))
+            hidden[r, frame(t)] = active.astype(BF16).astype(F32)
+
+    for r in range(2):
+        @pl.loop(0, times)
+        def _(t):
+            parts = []
+            lines = [
+                hidden[r, pl.ds(pl.multiple_of((t + kt) * width, width), width)] for kt in range(3)
+            ]
+            for kw in range(3):
+                parts += [shifted(line, kw - 1) for line in lines]
+            at = pl.ds(pl.multiple_of(t * width, width), width)
+            for i, pair in enumerate(pairs(parts)):
+                patches[r, at, i * 2 * small : (i + 1) * 2 * small] = pair
+
+    ring_got(1, 3)
+
+    for r in range(2):
+        total = None
+        for r_in in range(2):
+            kh = r_in - r + 1
+            term = lax.dot_general(
+                patches[r_in], mix_all[:, kh * span : (kh + 1) * span],
+                (((1,), (1,)), ((), ())), preferred_element_type=F32,
+            )
+            total = term if total is None else total + term
+        for t in range(times):
+            for c in range(4):
+                low = t * width + c * cols
+                part_d[c, t, r] = total[low : low + cols].astype(BF16)
+
+    def exchange(i, part, got):
+        return [
+            remote(part.at[target], got.at[j], out_send.at[i + j], out_recv.at[i + j], me, sibling)
+            for j, target in enumerate((sibling, diagonal))
+        ]
+
+    def add_and_cross(i, part, got, summed, last, first_copies):
+        for copy in first_copies:
+            copy.wait_recv()
+        summed[...] = (part[across].astype(F32) + got[1].astype(F32)).astype(BF16)
+        copy = remote(summed, last, out_send.at[i + 2], out_recv.at[i + 2], me, across)
+        copy.start()
+        return copy
+
+    def finish(part, got, last, copy, out):
+        copy.wait_recv()
+        out[...] = (part[q].astype(F32) + got[0].astype(F32) + last[...].astype(F32)).astype(BF16)
+
+    out_d = exchange(0, part_d, got_d)
+    for copy in out_d:
+        copy.start()
+
+    for r in range(2):
+        total = None
+        for r_in in range(2):
+            kh = r - r_in + 1
+            term = jnp.dot(
+                cots[r_in], mix_all[:, kh * span : (kh + 1) * span], preferred_element_type=F32
+            )
+            total = term if total is None else total + term
+        spread[r] = total
+
+    cross_d = add_and_cross(0, part_d, got_d, sum_d, last_d, out_d)
+
+    for r in range(2):
+        lines = []
+        for t in range(times + 1):
+            gradient = None
+            for kw in range(3):
+                part = None
+                for kt in range(3):
+                    low = (kw * 3 + kt) * small
+                    piece = spread[r, frame(t + 2 - kt), low : low + small]
+                    part = piece if part is None else part + piece
+                part = shifted(part, 1 - kw)
+                gradient = part if gradient is None else gradient + part
+            value = before[r, frame(t + 2)]
+            sigma = 1.0 / (1.0 + jnp.exp(-value))
+            gradient = gradient * sigma * (1.0 + value * (1.0 - sigma))
+            hidden[r, frame(t)] = gradient.astype(BF16).astype(F32)
+
+    for r in range(2):
+        for i in range(count):
+            lines = [hidden[r, frame(2 * i + kt)] for kt in range(3)]
+            for kw in range(3):
+                for j, pair in enumerate(pairs([shifted(line, 1 - kw) for line in lines])):
+                    grads[r, kw, frame(i), j * 2 * small : (j + 1) * 2 * small] = pair
+
+    for r in range(2):
+        total = None
+        for r_in in range(2):
+            kh = r - r_in + 1
+            for kw in range(3):
+                start = (kh * 3 + kw) * in_channels
+                term = jnp.dot(
+                    grads[r_in, kw], up_taps[:, start : start + in_channels],
+                    preferred_element_type=F32,
+                )
+                total = term if total is None else total + term
+        for i in range(count):
+            for c in range(4):
+                low = i * width + c * cols
+                part_g[c, i, r] = total[low : low + cols].astype(BF16)
+
+    out_g = exchange(3, part_g, got_g)
+    for copy in out_g:
+        copy.start()
+    finish(part_d, got_d, last_d, cross_d, decoded_ref)
+    cross_g = add_and_cross(3, part_g, got_g, sum_g, last_g, out_g)
+    finish(part_g, got_g, last_g, cross_g, grad_ref)
+    for copy in list(copies.values()) + halos + crossing + beside + passed:
+        copy.wait_send()
+    for copy in out_d + out_g + [cross_d, cross_g]:
+        copy.wait_send()
+
+
+def fused(frames, up_kernel, mix_kernel, cotangent):
+    n = lax.axis_size("tm")
+    count, height, cols, in_channels = frames.shape
+    times, channels = cotangent.shape[0], cotangent.shape[3]
+    width, small = 4 * cols, channels // 4
+    share = up_kernel.shape[1] // 4
+    q = lax.axis_index("col")
+    up_rows = lax.dynamic_slice_in_dim(up_kernel.T, q * share, share, 0)
+    up_rows = up_rows.reshape(share, 3, 9 * in_channels).transpose(1, 0, 2)
+    up_rows = up_rows.reshape(3 * share, 9 * in_channels)
+    mix_rows = mix_kernel.T
+    whole = pl.BlockSpec(memory_space=pltpu.VMEM)
+    d_block, g_block = (times, height, cols, channels), (count, height, cols, in_channels)
+    dma = pltpu.SemaphoreType.DMA
+    return pl.pallas_call(
+        functools.partial(fused_kernel, n),
+        out_shape=(
+            jax.ShapeDtypeStruct(d_block, BF16),
+            jax.ShapeDtypeStruct(g_block, BF16),
+        ),
+        in_specs=[whole] * 4,
+        out_specs=(whole, whole),
+        scratch_shapes=[
+            pltpu.VMEM((n,) + up_rows.shape, BF16),
+            pltpu.VMEM((channels, 30 * small), BF16),
+            pltpu.VMEM((4, count + 3, height, cols, in_channels), BF16),
+            pltpu.VMEM((4, times + 3, height, cols, channels), BF16),
+            pltpu.VMEM((4 * small, 9 * in_channels), BF16),
+            pltpu.VMEM((2, (count + 3) * width, 3 * in_channels), BF16),
+            pltpu.VMEM((2, (count + 3) * width, 4 * small), F32),
+            pltpu.VMEM((2, (times + 3) * width, small), F32),
+            pltpu.VMEM((2, (times + 3) * width, small), F32),
+            pltpu.VMEM((2, times * width, 10 * small), BF16),
+            pltpu.VMEM((2, (times + 3) * width, channels), BF16),
+            pltpu.VMEM((2, (times + 3) * width, 10 * small), F32),
+            pltpu.VMEM((2, 3, count * width, 4 * small), BF16),
+            pltpu.VMEM((4,) + d_block, BF16),
+            pltpu.VMEM((4,) + g_block, BF16),
+            pltpu.VMEM((2,) + d_block, BF16),
+            pltpu.VMEM((2,) + g_block, BF16),
+            pltpu.VMEM(d_block, BF16),
+            pltpu.VMEM(g_block, BF16),
+            pltpu.VMEM(d_block, BF16),
+            pltpu.VMEM(g_block, BF16),
+            dma((2, 2, n // 2)),
+            dma((2, 2, n // 2)),
+            dma((3,)),
+            dma((3,)),
+            dma((6,)),
+            dma((6,)),
+            dma((6,)),
+            dma((6,)),
+        ],
+        compiler_params=pltpu.CompilerParams(
+            collective_id=0, has_side_effects=True, vmem_limit_bytes=56 * 1024 * 1024
+        ),
+    )(up_rows, mix_rows, frames, cotangent)
+
+
 def solution(mesh):
     placed = (P("tm", None, "col", None), P(None, "tm"), P(None, "tm"), P("tm", None, "col", None))
+    small = mesh.shape["tm"] == 8 and mesh.shape["col"] == 4
     return jax.shard_map(
-        shards,
+        fused if small else shards,
         mesh=mesh,
         in_specs=placed,
         out_specs=(P("tm", None, "col", None), P("tm", None, "col", None)),

time: 236 us -> 57.7 us (0.24); the launches traced: 233 us -> 57.5 us
  waiting for transfers between devices: 121 us -> 0 us
  Pallas kernels: 0 us -> 52.8 us
  matrix products: 43.7 us -> 0 us
  starting transfers between devices: 28.7 us -> 0 us
  local copies, waits for them, and re-layouts: 19.1 us -> 4.02 us
  between operations: 15.6 us -> 0.66 us
  other arithmetic: 5.54 us -> 0 us
    all_gather x2 -> x0, waiting for transfers between devices: 112 us -> none  [forward_pass(): lax.all_gather(kernel, 'tm', axis=1, tiled=True)]
    pallas_call x0 -> x1, Pallas kernels: none -> 52.8 us  [fused(): pl.pallas_call(functools.partial(fused_kernel, n), out_shape=(jax.ShapeDt...]
    dot_general x108 -> x0, matrix products: 43.7 us -> none  [the longest x54 21 us: transposed(): lax.dot_general(rows, matrix, (((1,), (1,)), ((), ())), preferred_element...]
    ppermute x12 -> x0, starting transfers between devices: 28.6 us -> none  [the longest x4 11.8 us: with_halo(): lax.ppermute(lax.slice_in_dim(block, block.shape[dim] - width, None, axis...]
    all_gather x2 -> x0, local copies, waits for them, and re-layouts: 12.9 us -> none  [forward_pass(): lax.all_gather(kernel, 'tm', axis=1, tiled=True)]
    ppermute x12 -> x0, waiting for transfers between devices: 7.54 us -> none  [the longest x4 5.69 us: from_behind(): return lax.ppermute(array, axis, pairs)]
    concatenate x9 -> x0, other arithmetic: 5.21 us -> none  [the longest x7 4.23 us: with_halo(): block = jnp.concatenate([low, block, high], axis=dim)]
    slice x13 -> x0, local copies, waits for them, and re-layouts: 5.06 us -> none  [the longest x6 3.38 us: window(): padded[first:first + count, row_low:row_low + height, col_low:col_low + w...]
  transfers between devices with their start and end apart: 14 -> 0, of which waited for: 5 -> 0; matrix products, arithmetic and copies ran while one was open for 16% -> 0% of each run, Pallas kernels for 0% -> 0%
where the time goes in v1:
time: 57.7 us; the launch traced here: 57.5 us
  Pallas kernels  52.8 us (92%)
  local copies, waits for them, and re-layouts  4.02 us (7%)
  between operations  0.66 us (1%)
    pallas_call x1, Pallas kernels, fused(): pl.pallas_call(functools.partial(fused_kernel, n), out_shape=(jax.ShapeDt...  52.8 us
    unnamed x6, local copies, waits for them, and re-layouts  3.35 us

profile of v1, /device:TPU:0, one launch (start us, length us, event | category | flops | bytes accessed | tf_op | source)
XLA Modules:
  0.0 57.5 jit_solution(9694730540648871526)
XLA Ops:
  0.6 0.0 copy-start
  0.6 1.1 %copy-done = bf16[10368,32]{0,1:T(8,128)(2,1)S(1)} copy-done((bf16[10368,32]{0,1:T(8,128)(2,1)S(1)}, bf16[10368,32]{0,1:T(8,128)(2,1)}, u32[]{:S(2)}) %copy-start) | copy-done | bytes 663576
  1.7 0.7 %constant_dynamic-slice_fusion = bf16[10368,8]{0,1:T(8,128)(2,1)} fusion(bf16[10368,32]{0,1:T(8,128)(2,1)S(1)} %copy-done, s32[]{:T(128)S(6)} %select_n.3), kind=kLoop, calls=%fused_computation | loop fusion | bytes 331780 | tf_op jit(solution)/shard_map/dynamic-slice
  2.4 52.8 %shard_map.59 = (bf16[6,2,24,256]{3,2,1,0:T(8,128)(2,1)}, bf16[3,2,24,384]{3,2,1,0:T(8,128)(2,1)}) custom-call(bf16[24,3456]{1,0:T(8,128)(2,1)} %bitcast.8, bf16[32,6912]{1,0:T(8,128)(2,1)} %bitcast.9, bf16[3,2,24,384]{3,2,1,0:T(8,128)(2,1)} %frames_ref.1, bf16[6,2,24,256]{3,2,1,0:T(8,128)(2,1)} %cot_ref.1), custom_call_target="tpu_custom_call" | custom-call | tf_op jit(solution)/shard_map/pallas_call | solution.py:526
  55.2 0.0 copy-start.1
  55.2 1.6 %copy.8 = bf16[6,2,24,256]{3,2,1,0:T(8,128)(2,1)} copy(bf16[6,2,24,256]{3,2,1,0:T(8,128)(2,1)} %get-tuple-element.4) | data formatting | bytes 294912
  56.8 0.0 copy-done.1
  56.8 0.6 %copy.9 = bf16[3,2,24,384]{3,2,1,0:T(8,128)(2,1)} copy(bf16[3,2,24,384]{3,2,1,0:T(8,128)(2,1)S(1)} %copy-done.1) | data formatting | bytes 221184
Async XLA Ops:
  0.6 1.1 %copy-start = (bf16[10368,32]{0,1:T(8,128)(2,1)S(1)}, bf16[10368,32]{0,1:T(8,128)(2,1)}, u32[]{:S(2)}) copy-start(bf16[10368,32]{0,1:T(8,128)(2,1)} %param.5) | copy-start | bytes 1990660
  55.2 1.6 %copy-start.1 = (bf16[3,2,24,384]{3,2,1,0:T(8,128)(2,1)S(1)}, bf16[3,2,24,384]{3,2,1,0:T(8,128)(2,1)}, u32[]{:S(2)}) copy-start(bf16[3,2,24,384]{3,2,1,0:T(8,128)(2,1)} %get-tuple-element.5) | copy-start | bytes 331780

commit v2 on v1

--- a/solution.py
+++ b/solution.py
@@ -171,6 +171,7 @@
 MESH_ID = pl.DeviceIdType.MESH
 BF16 = jnp.bfloat16
 F32 = jnp.float32
+HEIGHTS = (1, 0, 2)
 
 
 def shifted(rows, by):
@@ -200,7 +201,7 @@
 
 def fused_kernel(
     n, up_ref, mix_ref, frames_ref, cot_ref, decoded_ref, grad_ref,
-    up_all, mix_all, frames_all, cot_all, up_taps, inputs, raw, before, hidden, patches,
+    up_all, mix_all, frames_all, cot_all, up_taps, inputs, raw, before, hidden, patches, decoding,
     cots, spread, grads, part_d, part_g, got_d, got_g, sum_d, sum_g, last_d, last_g,
     ring_send, ring_recv, halo_send, halo_recv, col_send, col_recv, out_send, out_recv,
 ):
@@ -218,7 +219,6 @@
     width = 4 * cols
     small = channels // 4
     rows = mix_ref.shape[0]
-    span = 9 * small + small
 
     def remote(src, dst, send, recv, tm, col):
         return pltpu.make_async_remote_copy(
@@ -229,6 +229,70 @@
     barrier = pltpu.get_barrier_semaphore()
     for tm, col in ((left, q), (right, q), (after, q), (ahead, q), (me, sibling), (me, across)):
         pl.semaphore_signal(barrier, inc=1, device_id=(tm, col), device_id_type=MESH_ID)
+
+    taken = 3 * in_channels
+    row = lax.broadcasted_iota(jnp.int32, (24, rows), 0)
+    column = lax.broadcasted_iota(jnp.int32, (24, rows), 1)
+    picks = [
+        jnp.where((row // 8 == kt) & (column == 8 * q + row % 8), 1.0, 0.0).astype(BF16)
+        for kt in range(3)
+    ]
+    for tap_h in HEIGHTS:
+        picked = None
+        for kt in range(3):
+            start = (kt * 3 + tap_h) * taken
+            term = jnp.dot(
+                picks[kt], up_ref[:, start : start + taken], preferred_element_type=F32
+            )
+            picked = term if picked is None else picked + term
+        up_all[tap_h, me] = picked.astype(BF16)
+    pl.semaphore_wait(barrier, 6)
+
+    def ring(direction, kind, tap_h, step):
+        owner = ring_tm((place + (n - step if direction == 0 else step)) % n, n)
+        target = right if direction == 0 else left
+        ref = up_all.at[tap_h, owner] if kind == 0 else mix_all.at[
+            tap_h, pl.ds(pl.multiple_of(owner * rows, rows), rows)
+        ]
+        index = (direction, kind, tap_h, step)
+        return remote(ref, ref, ring_send.at[index], ring_recv.at[index], target, q)
+
+    def steps_of(direction, kind):
+        return n // 2 if direction == kind else n // 2 - 1
+
+    copies = {}
+
+    def ring_start(kind, tap_h, step):
+        for direction in range(2):
+            if step < steps_of(direction, kind):
+                copy = ring(direction, kind, tap_h, step)
+                copies[direction, kind, tap_h, step] = copy
+                copy.start()
+
+    def ring_got(kind, tap_h, step):
+        for direction in range(2):
+            if step < steps_of(direction, kind):
+                copies[direction, kind, tap_h, step].wait_recv()
+
+    def ring_pass(kind, step):
+        for tap_h in HEIGHTS:
+            ring_got(kind, tap_h, step)
+            ring_start(kind, tap_h, step + 1)
+
+    for tap_h in HEIGHTS:
+        ring_start(0, tap_h, 0)
+    halos = [
+        remote(frames_ref.at[count - 2 : count], frames_all.at[q, 0:2],
+               halo_send.at[0], halo_recv.at[0], after, q),
+        remote(frames_ref.at[0:1], frames_all.at[q, count + 2 : count + 3],
+               halo_send.at[1], halo_recv.at[1], ahead, q),
+        remote(cot_ref.at[0:3], cot_all.at[q, times : times + 3],
+               halo_send.at[2], halo_recv.at[2], ahead, q),
+    ]
+    for copy in halos:
+        copy.start()
+    frames_all[q, 2 : 2 + count] = frames_ref[...]
+    cot_all[q, 0:times] = cot_ref[...]
 
     source = lax.broadcasted_iota(jnp.int32, (channels, 2 * small), 0)
     lane = lax.broadcasted_iota(jnp.int32, (channels, 2 * small), 1)
@@ -237,7 +301,7 @@
     first = jnp.where((source == wanted) & (lane < small), 1.0, 0.0).astype(BF16)
     second = jnp.where((source == wanted) & (lane >= small), 1.0, 0.0).astype(BF16)
     mine = pl.ds(pl.multiple_of(me * rows, rows), rows)
-    for tap_h in range(3):
+    for tap_h in HEIGHTS:
         order = [(kt * 3 + tap_h) * 3 + kw for kw in range(3) for kt in range(3)]
         for i in range(0, 10, 2):
             picked = jnp.dot(
@@ -249,52 +313,10 @@
                     mix_ref[:, order[i + 1] * channels : (order[i + 1] + 1) * channels], second,
                     preferred_element_type=F32,
                 )
-            start = tap_h * span + i * small
-            mix_all[mine, start : start + 2 * small] = picked.astype(BF16)
-    up_all[me] = up_ref[...]
-    frames_all[q, 2 : 2 + count] = frames_ref[...]
-    cot_all[q, 0:times] = cot_ref[...]
-    pl.semaphore_wait(barrier, 6)
-
-    def ring(direction, kind, step):
-        owner = ring_tm((place + (n - step if direction == 0 else step)) % n, n)
-        target = right if direction == 0 else left
-        ref = up_all.at[owner] if kind == 0 else mix_all.at[
-            pl.ds(pl.multiple_of(owner * rows, rows), rows)
-        ]
-        return remote(
-            ref, ref, ring_send.at[direction, kind, step], ring_recv.at[direction, kind, step],
-            target, q,
-        )
-
-    def steps_of(direction, kind):
-        return n // 2 if direction == kind else n // 2 - 1
-
-    copies = {}
-
-    def ring_start(kind, step):
-        for direction in range(2):
-            if step < steps_of(direction, kind):
-                copies[direction, kind, step] = ring(direction, kind, step)
-                copies[direction, kind, step].start()
-
-    def ring_got(kind, step):
-        for direction in range(2):
-            if step < steps_of(direction, kind):
-                copies[direction, kind, step].wait_recv()
-
-    ring_start(0, 0)
-    halos = [
-        remote(frames_ref.at[count - 2 : count], frames_all.at[q, 0:2],
-               halo_send.at[0], halo_recv.at[0], after, q),
-        remote(frames_ref.at[0:1], frames_all.at[q, count + 2 : count + 3],
-               halo_send.at[1], halo_recv.at[1], ahead, q),
-        remote(cot_ref.at[0:3], cot_all.at[q, times : times + 3],
-               halo_send.at[2], halo_recv.at[2], ahead, q),
-    ]
-    for copy in halos:
-        copy.start()
-    ring_start(1, 0)
+            mix_all[tap_h, mine, i * small : (i + 2) * small] = picked.astype(BF16)
+    ring_pass(0, 0)
+    for tap_h in HEIGHTS:
+        ring_start(1, tap_h, 0)
     for copy in halos:
         copy.wait_recv()
 
@@ -317,10 +339,7 @@
     ]
     for copy in crossing + beside:
         copy.start()
-    ring_got(0, 0)
-    ring_start(0, 1)
-    ring_got(1, 0)
-    ring_start(1, 1)
+    ring_pass(0, 1)
     for copy in crossing:
         copy.wait_recv()
     passed = [
@@ -329,10 +348,8 @@
     ]
     for copy in passed:
         copy.start()
-    ring_got(0, 1)
-    ring_start(0, 2)
-    ring_got(1, 1)
-    ring_start(1, 2)
+    ring_pass(1, 0)
+    ring_pass(0, 2)
     for copy in beside + passed:
         copy.wait_recv()
 
@@ -352,32 +369,24 @@
             line = jnp.concatenate([cot_all[c, t, r].astype(F32) for c in range(4)], axis=0)
             cots[r, pl.ds(pl.multiple_of(t * width, width), width)] = line.astype(BF16)
 
-    ring_got(0, 2)
-    ring_start(0, 3)
-    ring_got(1, 2)
-    ring_start(1, 3)
-    ring_got(0, 3)
-
-    taken = 9 * in_channels
-    for kt in range(3):
-        for start in range(0, taken, in_channels):
-            part = up_all[:, kt * 8 : kt * 8 + 8, start : start + in_channels].astype(F32)
-            up_taps[kt * small : (kt + 1) * small, start : start + in_channels] = part.reshape(
-                small, in_channels
-            ).astype(BF16)
-    up_taps[3 * small : 4 * small] = jnp.zeros((small, taken), BF16)
-
-    wide = 3 * in_channels
-    for r in range(2):
-        total = None
-        for r_in in range(2):
-            kh = r_in - r + 1
-            term = lax.dot_general(
-                inputs[r_in], up_taps[:, kh * wide : (kh + 1) * wide],
-                (((1,), (1,)), ((), ())), preferred_element_type=F32,
-            )
-            total = term if total is None else total + term
-        raw[r] = total
+    ring_pass(1, 1)
+
+    for step, kh in enumerate(HEIGHTS):
+        ring_got(0, kh, 3)
+        for kt in range(3):
+            part = up_all[kh, :, kt * 8 : kt * 8 + 8, :].astype(F32)
+            up_taps[kh, kt * small : (kt + 1) * small] = part.reshape(small, taken).astype(BF16)
+        up_taps[kh, 3 * small : 4 * small] = jnp.zeros((small, taken), BF16)
+        for r in range(2):
+            r_in = r + kh - 1
+            if 0 <= r_in < 2:
+                term = lax.dot_general(
+                    inputs[r_in], up_taps[kh], (((1,), (1,)), ((), ())),
+                    preferred_element_type=F32,
+                )
+                raw[r] = term if step == 0 else raw[r] + term
+        if step == 0:
+            ring_pass(1, 2)
 
     def frame(t):
         return slice(t * width, (t + 1) * width)
@@ -407,27 +416,36 @@
             for i, pair in enumerate(pairs(parts)):
                 patches[r, at, i * 2 * small : (i + 1) * 2 * small] = pair
 
-    ring_got(1, 3)
-
-    for r in range(2):
-        total = None
-        for r_in in range(2):
-            kh = r_in - r + 1
-            term = lax.dot_general(
-                patches[r_in], mix_all[:, kh * span : (kh + 1) * span],
-                (((1,), (1,)), ((), ())), preferred_element_type=F32,
-            )
-            total = term if total is None else total + term
-        for t in range(times):
-            for c in range(4):
-                low = t * width + c * cols
-                part_d[c, t, r] = total[low : low + cols].astype(BF16)
-
     def exchange(i, part, got):
         return [
             remote(part.at[target], got.at[j], out_send.at[i + j], out_recv.at[i + j], me, sibling)
             for j, target in enumerate((sibling, diagonal))
         ]
+
+    out_d = exchange(0, part_d, got_d)
+    for step, kh in enumerate(HEIGHTS):
+        ring_got(1, kh, 3)
+        for r in range(2):
+            r_in = r + kh - 1
+            if 0 <= r_in < 2:
+                term = lax.dot_general(
+                    patches[r_in], mix_all[kh], (((1,), (1,)), ((), ())),
+                    preferred_element_type=F32,
+                )
+                decoding[r] = term if step == 0 else decoding[r] + term
+        if step == 2:
+            for r in range(2):
+                for t in range(times):
+                    for c in range(4):
+                        low = t * width + c * cols
+                        part_d[c, t, r] = decoding[r, low : low + cols].astype(BF16)
+            for copy in out_d:
+                copy.start()
+        for r in range(2):
+            r_in = r - kh + 1
+            if 0 <= r_in < 2:
+                term = jnp.dot(cots[r_in], mix_all[kh], preferred_element_type=F32)
+                spread[r] = term if step == 0 else spread[r] + term
 
     def add_and_cross(i, part, got, summed, last, first_copies):
         for copy in first_copies:
@@ -440,20 +458,6 @@
     def finish(part, got, last, copy, out):
         copy.wait_recv()
         out[...] = (part[q].astype(F32) + got[0].astype(F32) + last[...].astype(F32)).astype(BF16)
-
-    out_d = exchange(0, part_d, got_d)
-    for copy in out_d:
-        copy.start()
-
-    for r in range(2):
-        total = None
-        for r_in in range(2):
-            kh = r - r_in + 1
-            term = jnp.dot(
-                cots[r_in], mix_all[:, kh * span : (kh + 1) * span], preferred_element_type=F32
-            )
-            total = term if total is None else total + term
-        spread[r] = total
 
     cross_d = add_and_cross(0, part_d, got_d, sum_d, last_d, out_d)
 
@@ -486,9 +490,9 @@
         for r_in in range(2):
             kh = r - r_in + 1
             for kw in range(3):
-                start = (kh * 3 + kw) * in_channels
+                start = kw * in_channels
                 term = jnp.dot(
-                    grads[r_in, kw], up_taps[:, start : start + in_channels],
+                    grads[r_in, kw], up_taps[kh, :, start : start + in_channels],
                     preferred_element_type=F32,
                 )
                 total = term if total is None else total + term
@@ -514,12 +518,7 @@
     count, height, cols, in_channels = frames.shape
     times, channels = cotangent.shape[0], cotangent.shape[3]
     width, small = 4 * cols, channels // 4
-    share = up_kernel.shape[1] // 4
-    q = lax.axis_index("col")
-    up_rows = lax.dynamic_slice_in_dim(up_kernel.T, q * share, share, 0)
-    up_rows = up_rows.reshape(share, 3, 9 * in_channels).transpose(1, 0, 2)
-    up_rows = up_rows.reshape(3 * share, 9 * in_channels)
-    mix_rows = mix_kernel.T
+    up_rows, mix_rows = up_kernel.T, mix_kernel.T
     whole = pl.BlockSpec(memory_space=pltpu.VMEM)
     d_block, g_block = (times, height, cols, channels), (count, height, cols, in_channels)
     dma = pltpu.SemaphoreType.DMA
@@ -532,16 +531,17 @@
         in_specs=[whole] * 4,
         out_specs=(whole, whole),
         scratch_shapes=[
-            pltpu.VMEM((n,) + up_rows.shape, BF16),
-            pltpu.VMEM((channels, 30 * small), BF16),
+            pltpu.VMEM((3, n, 24, 3 * in_channels), BF16),
+            pltpu.VMEM((3, channels, 10 * small), BF16),
             pltpu.VMEM((4, count + 3, height, cols, in_channels), BF16),
             pltpu.VMEM((4, times + 3, height, cols, channels), BF16),
-            pltpu.VMEM((4 * small, 9 * in_channels), BF16),
+            pltpu.VMEM((3, 4 * small, 3 * in_channels), BF16),
             pltpu.VMEM((2, (count + 3) * width, 3 * in_channels), BF16),
             pltpu.VMEM((2, (count + 3) * width, 4 * small), F32),
             pltpu.VMEM((2, (times + 3) * width, small), F32),
             pltpu.VMEM((2, (times + 3) * width, small), F32),
             pltpu.VMEM((2, times * width, 10 * small), BF16),
+            pltpu.VMEM((2, times * width, channels), F32),
             pltpu.VMEM((2, (times + 3) * width, channels), BF16),
             pltpu.VMEM((2, (times + 3) * width, 10 * small), F32),
             pltpu.VMEM((2, 3, count * width, 4 * small), BF16),
@@ -553,8 +553,8 @@
             pltpu.VMEM(g_block, BF16),
             pltpu.VMEM(d_block, BF16),
             pltpu.VMEM(g_block, BF16),
-            dma((2, 2, n // 2)),
-            dma((2, 2, n // 2)),
+            dma((2, 2, 3, n // 2)),
+            dma((2, 2, 3, n // 2)),
             dma((3,)),
             dma((3,)),
             dma((6,)),

time: 57.7 us -> 57.6 us (level)
  local copies, waits for them, and re-layouts: 4.02 us -> 2.26 us
  Pallas kernels: 52.8 us -> 54.5 us
    pallas_call x1, Pallas kernels: 52.8 us -> 54.5 us  [fused(): pl.pallas_call(functools.partial(fused_kernel, n), out_shape=(jax.ShapeDt...]
    unnamed x6 -> x4, local copies, waits for them, and re-layouts: 3.35 us -> 2.26 us
    another operation x1 -> x0, local copies, waits for them, and re-layouts: 0.67 us -> none
where the time goes in v2:
time: 57.6 us; the launch traced here: 57.4 us
  Pallas kernels  54.5 us (95%)
  local copies, waits for them, and re-layouts  2.26 us (4%)
  between operations  0.65 us (1%)
    pallas_call x1, Pallas kernels, fused(): pl.pallas_call(functools.partial(fused_kernel, n), out_shape=(jax.ShapeDt...  54.5 us
    unnamed x4, local copies, waits for them, and re-layouts  2.26 us

profile of v2, /device:TPU:0, one launch (start us, length us, event | category | flops | bytes accessed | tf_op | source)
XLA Modules:
  0.0 57.4 jit_solution(6257338085929391801)
XLA Ops:
  0.6 54.5 %shard_map.59 = (bf16[6,2,24,256]{3,2,1,0:T(8,128)(2,1)}, bf16[3,2,24,384]{3,2,1,0:T(8,128)(2,1)}) custom-call(bf16[32,10368]{1,0:T(8,128)(2,1)} %bitcast.2, bf16[32,6912]{1,0:T(8,128)(2,1)} %bitcast.3, bf16[3,2,24,384]{3,2,1,0:T(8,128)(2,1)} %frames_ref.1, bf16[6,2,24,256]{3,2,1,0:T(8,128)(2,1)} %cot_ref.1), custom_call_target="tpu_custom_call" | custom-call | tf_op jit(solution)/shard_map/pallas_call | solution.py:525
  55.2 0.0 copy-start
  55.2 1.6 %copy.8 = bf16[6,2,24,256]{3,2,1,0:T(8,128)(2,1)} copy(bf16[6,2,24,256]{3,2,1,0:T(8,128)(2,1)} %get-tuple-element.4) | data formatting | bytes 294912
  56.8 0.0 copy-done
  56.8 0.6 %copy.9 = bf16[3,2,24,384]{3,2,1,0:T(8,128)(2,1)} copy(bf16[3,2,24,384]{3,2,1,0:T(8,128)(2,1)S(1)} %copy-done) | data formatting | bytes 221184
Async XLA Ops:
  55.2 1.6 %copy-start = (bf16[3,2,24,384]{3,2,1,0:T(8,128)(2,1)S(1)}, bf16[3,2,24,384]{3,2,1,0:T(8,128)(2,1)}, u32[]{:S(2)}) copy-start(bf16[3,2,24,384]{3,2,1,0:T(8,128)(2,1)} %get-tuple-element.5) | copy-start | bytes 331780

commit v3 on v2

--- a/solution.py
+++ b/solution.py
@@ -279,8 +279,15 @@
             ring_got(kind, tap_h, step)
             ring_start(kind, tap_h, step + 1)
 
-    for tap_h in HEIGHTS:
-        ring_start(0, tap_h, 0)
+    own = [
+        remote(src, dst, col_send.at[i], col_recv.at[i], me, col)
+        for i, (src, dst, col) in enumerate((
+            (frames_ref, frames_all.at[q, 2 : 2 + count], across),
+            (cot_ref, cot_all.at[q, 0:times], across),
+            (frames_ref, frames_all.at[q, 2 : 2 + count], sibling),
+            (cot_ref, cot_all.at[q, 0:times], sibling),
+        ))
+    ]
     halos = [
         remote(frames_ref.at[count - 2 : count], frames_all.at[q, 0:2],
                halo_send.at[0], halo_recv.at[0], after, q),
@@ -290,6 +297,10 @@
                halo_send.at[2], halo_recv.at[2], ahead, q),
     ]
     for copy in halos:
+        copy.start()
+    for tap_h in HEIGHTS:
+        ring_start(0, tap_h, 0)
+    for copy in own:
         copy.start()
     frames_all[q, 2 : 2 + count] = frames_ref[...]
     cot_all[q, 0:times] = cot_ref[...]
@@ -329,28 +340,33 @@
         frames_all[q, count + 2 : count + 3] = jnp.zeros((1,) + frames_ref.shape[1:], BF16)
         cot_all[q, times : times + 3] = jnp.zeros((3,) + cot_ref.shape[1:], BF16)
 
+    edges = (
+        frames_all.at[q, 0:2], frames_all.at[q, count + 2 : count + 3],
+        cot_all.at[q, times : times + 3],
+    )
     crossing = [
-        remote(ref.at[q], ref.at[q], col_send.at[i], col_recv.at[i], me, across)
-        for i, ref in enumerate((frames_all, cot_all))
+        remote(ref, ref, col_send.at[4 + i], col_recv.at[4 + i], me, across)
+        for i, ref in enumerate(edges)
     ]
     beside = [
-        remote(ref.at[q], ref.at[q], col_send.at[2 + i], col_recv.at[2 + i], me, sibling)
-        for i, ref in enumerate((frames_all, cot_all))
+        remote(ref, ref, col_send.at[7 + i], col_recv.at[7 + i], me, sibling)
+        for i, ref in enumerate(edges)
     ]
     for copy in crossing + beside:
         copy.start()
     ring_pass(0, 1)
-    for copy in crossing:
+    ring_pass(1, 0)
+    ring_pass(0, 2)
+    for copy in own[:2] + crossing:
         copy.wait_recv()
     passed = [
-        remote(ref.at[across], ref.at[across], col_send.at[4 + i], col_recv.at[4 + i], me, sibling)
+        remote(ref.at[across], ref.at[across], col_send.at[10 + i], col_recv.at[10 + i], me, sibling)
         for i, ref in enumerate((frames_all, cot_all))
     ]
     for copy in passed:
         copy.start()
-    ring_pass(1, 0)
-    ring_pass(0, 2)
-    for copy in beside + passed:
+    ring_pass(1, 1)
+    for copy in own[2:] + beside + passed:
         copy.wait_recv()
 
     @pl.loop(0, count + 3)
@@ -368,8 +384,6 @@
         for r in range(2):
             line = jnp.concatenate([cot_all[c, t, r].astype(F32) for c in range(4)], axis=0)
             cots[r, pl.ds(pl.multiple_of(t * width, width), width)] = line.astype(BF16)
-
-    ring_pass(1, 1)
 
     for step, kh in enumerate(HEIGHTS):
         ring_got(0, kh, 3)
@@ -485,6 +499,7 @@
                 for j, pair in enumerate(pairs([shifted(line, 1 - kw) for line in lines])):
                     grads[r, kw, frame(i), j * 2 * small : (j + 1) * 2 * small] = pair
 
+    out_g = []
     for r in range(2):
         total = None
         for r_in in range(2):
@@ -499,17 +514,22 @@
         for i in range(count):
             for c in range(4):
                 low = i * width + c * cols
-                part_g[c, i, r] = total[low : low + cols].astype(BF16)
-
-    out_g = exchange(3, part_g, got_g)
-    for copy in out_g:
-        copy.start()
+                part_g[r, c, i] = total[low : low + cols].astype(BF16)
+        out_g.append(exchange(3 + 3 * r, part_g.at[r], got_g.at[r]))
+        for copy in out_g[r]:
+            copy.start()
     finish(part_d, got_d, last_d, cross_d, decoded_ref)
-    cross_g = add_and_cross(3, part_g, got_g, sum_g, last_g, out_g)
-    finish(part_g, got_g, last_g, cross_g, grad_ref)
-    for copy in list(copies.values()) + halos + crossing + beside + passed:
+    cross_g = [
+        add_and_cross(
+            3 + 3 * r, part_g.at[r], got_g.at[r], sum_g.at[r], last_g.at[r], out_g[r]
+        )
+        for r in range(2)
+    ]
+    for r in range(2):
+        finish(part_g.at[r], got_g.at[r], last_g.at[r], cross_g[r], grad_ref.at[:, r])
+    for copy in list(copies.values()) + halos + own + crossing + beside + passed:
         copy.wait_send()
-    for copy in out_d + out_g + [cross_d, cross_g]:
+    for copy in out_d + out_g[0] + out_g[1] + [cross_d] + cross_g:
         copy.wait_send()
 
 
@@ -521,6 +541,7 @@
     up_rows, mix_rows = up_kernel.T, mix_kernel.T
     whole = pl.BlockSpec(memory_space=pltpu.VMEM)
     d_block, g_block = (times, height, cols, channels), (count, height, cols, in_channels)
+    g_half = (count, cols, in_channels)
     dma = pltpu.SemaphoreType.DMA
     return pl.pallas_call(
         functools.partial(fused_kernel, n),
@@ -546,21 +567,21 @@
             pltpu.VMEM((2, (times + 3) * width, 10 * small), F32),
             pltpu.VMEM((2, 3, count * width, 4 * small), BF16),
             pltpu.VMEM((4,) + d_block, BF16),
-            pltpu.VMEM((4,) + g_block, BF16),
+            pltpu.VMEM((2, 4) + g_half, BF16),
             pltpu.VMEM((2,) + d_block, BF16),
-            pltpu.VMEM((2,) + g_block, BF16),
+            pltpu.VMEM((2, 2) + g_half, BF16),
             pltpu.VMEM(d_block, BF16),
-            pltpu.VMEM(g_block, BF16),
+            pltpu.VMEM((2,) + g_half, BF16),
             pltpu.VMEM(d_block, BF16),
-            pltpu.VMEM(g_block, BF16),
+            pltpu.VMEM((2,) + g_half, BF16),
             dma((2, 2, 3, n // 2)),
             dma((2, 2, 3, n // 2)),
             dma((3,)),
             dma((3,)),
-            dma((6,)),
-            dma((6,)),
-            dma((6,)),
-            dma((6,)),
+            dma((12,)),
+            dma((12,)),
+            dma((9,)),
+            dma((9,)),
         ],
         compiler_params=pltpu.CompilerParams(
             collective_id=0, has_side_effects=True, vmem_limit_bytes=56 * 1024 * 1024

time: 57.6 us -> 54.6 us (0.948)
  Pallas kernels: 54.5 us -> 51.6 us
    pallas_call x1, Pallas kernels: 54.5 us -> 51.6 us  [fused(): pl.pallas_call(functools.partial(fused_kernel, n), out_shape=(jax.ShapeDt...]
where the time goes in v3:
time: 54.6 us; the launch traced here: 54.5 us
  Pallas kernels  51.6 us (95%)
  local copies, waits for them, and re-layouts  2.26 us (4%)
  between operations  0.65 us (1%)
    pallas_call x1, Pallas kernels, fused(): pl.pallas_call(functools.partial(fused_kernel, n), out_shape=(jax.ShapeDt...  51.6 us
    unnamed x4, local copies, waits for them, and re-layouts  2.26 us

profile of v3, /device:TPU:0, one launch (start us, length us, event | category | flops | bytes accessed | tf_op | source)
XLA Modules:
  0.0 54.5 jit_solution(5308474962481954592)
XLA Ops:
  0.6 51.6 %shard_map.59 = (bf16[6,2,24,256]{3,2,1,0:T(8,128)(2,1)}, bf16[3,2,24,384]{3,2,1,0:T(8,128)(2,1)}) custom-call(bf16[32,10368]{1,0:T(8,128)(2,1)} %bitcast.2, bf16[32,6912]{1,0:T(8,128)(2,1)} %bitcast.3, bf16[3,2,24,384]{3,2,1,0:T(8,128)(2,1)} %frames_ref.1, bf16[6,2,24,256]{3,2,1,0:T(8,128)(2,1)} %cot_ref.1), custom_call_target="tpu_custom_call" | custom-call | tf_op jit(solution)/shard_map/pallas_call | solution.py:546
  52.2 0.0 copy-start
  52.2 1.6 %copy.8 = bf16[6,2,24,256]{3,2,1,0:T(8,128)(2,1)} copy(bf16[6,2,24,256]{3,2,1,0:T(8,128)(2,1)} %get-tuple-element.4) | data formatting | bytes 294912
  53.8 0.0 copy-done
  53.8 0.6 %copy.9 = bf16[3,2,24,384]{3,2,1,0:T(8,128)(2,1)} copy(bf16[3,2,24,384]{3,2,1,0:T(8,128)(2,1)S(1)} %copy-done) | data formatting | bytes 221184
Async XLA Ops:
  52.2 1.6 %copy-start = (bf16[3,2,24,384]{3,2,1,0:T(8,128)(2,1)S(1)}, bf16[3,2,24,384]{3,2,1,0:T(8,128)(2,1)}, u32[]{:S(2)}) copy-start(bf16[3,2,24,384]{3,2,1,0:T(8,128)(2,1)} %get-tuple-element.5) | copy-start | bytes 331780

commit v4 on v3

--- a/solution.py
+++ b/solution.py
@@ -171,7 +171,7 @@
 MESH_ID = pl.DeviceIdType.MESH
 BF16 = jnp.bfloat16
 F32 = jnp.float32
-HEIGHTS = (1, 0, 2)
+TAPS_W = (1, 0, 2)
 
 
 def shifted(rows, by):
@@ -184,15 +184,6 @@
     return jnp.where(place == count - 1, 0.0, pltpu.roll(rows, count - 1, 0))
 
 
-def pairs(parts):
-    if len(parts) % 2:
-        parts = parts + [jnp.zeros_like(parts[0])]
-    return [
-        jnp.concatenate((parts[i], parts[i + 1]), axis=1).astype(BF16)
-        for i in range(0, len(parts), 2)
-    ]
-
-
 def ring_tm(place, n):
     half = place // (n // 2)
     level = place + half * (n - 1 - 2 * place)
@@ -201,8 +192,8 @@
 
 def fused_kernel(
     n, up_ref, mix_ref, frames_ref, cot_ref, decoded_ref, grad_ref,
-    up_all, mix_all, frames_all, cot_all, up_taps, inputs, raw, before, hidden, patches, decoding,
-    cots, spread, grads, part_d, part_g, got_d, got_g, sum_d, sum_g, last_d, last_g,
+    up_all, mix_all, frames_all, cot_all, up_taps, inputs, mix_taps, raw, before, patches, decoding,
+    cots, spread, gradient, grads, part_d, part_g, got_d, got_g, sum_d, sum_g, last_d, last_g,
     ring_send, ring_recv, halo_send, halo_recv, col_send, col_recv, out_send, out_recv,
 ):
     me, q = lax.axis_index("tm"), lax.axis_index("col")
@@ -230,31 +221,31 @@
     for tm, col in ((left, q), (right, q), (after, q), (ahead, q), (me, sibling), (me, across)):
         pl.semaphore_signal(barrier, inc=1, device_id=(tm, col), device_id_type=MESH_ID)
 
-    taken = 3 * in_channels
     row = lax.broadcasted_iota(jnp.int32, (24, rows), 0)
     column = lax.broadcasted_iota(jnp.int32, (24, rows), 1)
-    picks = [
-        jnp.where((row // 8 == kt) & (column == 8 * q + row % 8), 1.0, 0.0).astype(BF16)
-        for kt in range(3)
-    ]
-    for tap_h in HEIGHTS:
-        picked = None
-        for kt in range(3):
-            start = (kt * 3 + tap_h) * taken
-            term = jnp.dot(
-                picks[kt], up_ref[:, start : start + taken], preferred_element_type=F32
-            )
-            picked = term if picked is None else picked + term
-        up_all[tap_h, me] = picked.astype(BF16)
+    picked = None
+    for kt in range(3):
+        pick = jnp.where((row // 8 == kt) & (column == 8 * q + row % 8), 1.0, 0.0).astype(BF16)
+        term = jnp.dot(
+            pick, up_ref[:, kt * 9 * in_channels : (kt + 1) * 9 * in_channels],
+            preferred_element_type=F32,
+        )
+        picked = term if picked is None else picked + term
+    for kw in range(3):
+        for kh in range(3):
+            low = (kh * 3 + kw) * in_channels
+            up_all[kw, me, :, kh * in_channels : (kh + 1) * in_channels] = picked[
+                :, low : low + in_channels
+            ].astype(BF16)
     pl.semaphore_wait(barrier, 6)
 
-    def ring(direction, kind, tap_h, step):
+    def ring(direction, kind, tap_w, step):
         owner = ring_tm((place + (n - step if direction == 0 else step)) % n, n)
         target = right if direction == 0 else left
-        ref = up_all.at[tap_h, owner] if kind == 0 else mix_all.at[
-            tap_h, pl.ds(pl.multiple_of(owner * rows, rows), rows)
+        ref = up_all.at[tap_w, owner] if kind == 0 else mix_all.at[
+            tap_w, pl.ds(pl.multiple_of(owner * rows, rows), rows)
         ]
-        index = (direction, kind, tap_h, step)
+        index = (direction, kind, tap_w, step)
         return remote(ref, ref, ring_send.at[index], ring_recv.at[index], target, q)
 
     def steps_of(direction, kind):
@@ -262,22 +253,22 @@
 
     copies = {}
 
-    def ring_start(kind, tap_h, step):
+    def ring_start(kind, tap_w, step):
         for direction in range(2):
             if step < steps_of(direction, kind):
-                copy = ring(direction, kind, tap_h, step)
-                copies[direction, kind, tap_h, step] = copy
+                copy = ring(direction, kind, tap_w, step)
+                copies[direction, kind, tap_w, step] = copy
                 copy.start()
 
-    def ring_got(kind, tap_h, step):
+    def ring_got(kind, tap_w, step):
         for direction in range(2):
             if step < steps_of(direction, kind):
-                copies[direction, kind, tap_h, step].wait_recv()
+                copies[direction, kind, tap_w, step].wait_recv()
 
     def ring_pass(kind, step):
-        for tap_h in HEIGHTS:
-            ring_got(kind, tap_h, step)
-            ring_start(kind, tap_h, step + 1)
+        for tap_w in TAPS_W:
+            ring_got(kind, tap_w, step)
+            ring_start(kind, tap_w, step + 1)
 
     own = [
         remote(src, dst, col_send.at[i], col_recv.at[i], me, col)
@@ -296,10 +287,18 @@
         remote(cot_ref.at[0:3], cot_all.at[q, times : times + 3],
                halo_send.at[2], halo_recv.at[2], ahead, q),
     ]
-    for copy in halos:
-        copy.start()
-    for tap_h in HEIGHTS:
-        ring_start(0, tap_h, 0)
+
+    @pl.when(me < n - 1)
+    def _():
+        halos[0].start()
+
+    @pl.when(me > 0)
+    def _():
+        halos[1].start()
+        halos[2].start()
+
+    for tap_w in TAPS_W:
+        ring_start(0, tap_w, 0)
     for copy in own:
         copy.start()
     frames_all[q, 2 : 2 + count] = frames_ref[...]
@@ -312,28 +311,37 @@
     first = jnp.where((source == wanted) & (lane < small), 1.0, 0.0).astype(BF16)
     second = jnp.where((source == wanted) & (lane >= small), 1.0, 0.0).astype(BF16)
     mine = pl.ds(pl.multiple_of(me * rows, rows), rows)
-    for tap_h in HEIGHTS:
-        order = [(kt * 3 + tap_h) * 3 + kw for kw in range(3) for kt in range(3)]
-        for i in range(0, 10, 2):
-            picked = jnp.dot(
-                mix_ref[:, order[i] * channels : (order[i] + 1) * channels], first,
-                preferred_element_type=F32,
-            )
-            if i < 8:
-                picked = picked + jnp.dot(
-                    mix_ref[:, order[i + 1] * channels : (order[i + 1] + 1) * channels], second,
-                    preferred_element_type=F32,
-                )
-            mix_all[tap_h, mine, i * small : (i + 2) * small] = picked.astype(BF16)
+    def taken(order, pick):
+        lines = [
+            mix_ref[:, ((kt * 3 + kh) * 3 + kw) * channels : ((kt * 3 + kh) * 3 + kw + 1) * channels]
+            for kt, kh, kw in order
+        ]
+        return jnp.dot(jnp.concatenate(lines, axis=0), pick, preferred_element_type=F32)
+
+    for kw in TAPS_W:
+        low = taken([(0, 0, kw), (1, 0, kw), (2, 0, kw), (1, 2, kw)], first)
+        high = taken([(0, 1, kw), (1, 1, kw), (2, 1, kw), (0, 2, kw), (2, 2, kw)], second)
+        for i in range(5):
+            part = high[i * rows : (i + 1) * rows]
+            if i < 4:
+                part = part + low[i * rows : (i + 1) * rows]
+            mix_all[kw, mine, i * 2 * small : (i + 1) * 2 * small] = part.astype(BF16)
     ring_pass(0, 0)
-    for tap_h in HEIGHTS:
-        ring_start(1, tap_h, 0)
-    for copy in halos:
-        copy.wait_recv()
+    for tap_w in TAPS_W:
+        ring_start(1, tap_w, 0)
+
+    @pl.when(me > 0)
+    def _():
+        halos[0].wait_recv()
 
     @pl.when(me == 0)
     def _():
         frames_all[q, 0:2] = jnp.zeros((2,) + frames_ref.shape[1:], BF16)
+
+    @pl.when(me < n - 1)
+    def _():
+        halos[1].wait_recv()
+        halos[2].wait_recv()
 
     @pl.when(me == n - 1)
     def _():
@@ -371,64 +379,59 @@
 
     @pl.loop(0, count + 3)
     def _(t):
+        at = pl.ds(pl.multiple_of(t * width, width), width)
         for r in range(2):
             line = jnp.concatenate([frames_all[c, t, r].astype(F32) for c in range(4)], axis=0)
-            at = pl.ds(pl.multiple_of(t * width, width), width)
             for kw in range(3):
-                inputs[r, at, kw * in_channels : (kw + 1) * in_channels] = shifted(
+                inputs[kw, at, r * in_channels : (r + 1) * in_channels] = shifted(
                     line, kw - 1
                 ).astype(BF16)
 
     @pl.loop(0, times + 3)
     def _(t):
+        at = pl.ds(pl.multiple_of(t * width, width), width)
         for r in range(2):
             line = jnp.concatenate([cot_all[c, t, r].astype(F32) for c in range(4)], axis=0)
-            cots[r, pl.ds(pl.multiple_of(t * width, width), width)] = line.astype(BF16)
-
-    for step, kh in enumerate(HEIGHTS):
-        ring_got(0, kh, 3)
+            cots[at, r * channels : (r + 1) * channels] = line.astype(BF16)
+
+    pair = 2 * small
+    for step, kw in enumerate(TAPS_W):
+        ring_got(0, kw, 3)
         for kt in range(3):
-            part = up_all[kh, :, kt * 8 : kt * 8 + 8, :].astype(F32)
-            up_taps[kh, kt * small : (kt + 1) * small] = part.reshape(small, taken).astype(BF16)
-        up_taps[kh, 3 * small : 4 * small] = jnp.zeros((small, taken), BF16)
-        for r in range(2):
-            r_in = r + kh - 1
-            if 0 <= r_in < 2:
-                term = lax.dot_general(
-                    inputs[r_in], up_taps[kh], (((1,), (1,)), ((), ())),
-                    preferred_element_type=F32,
-                )
-                raw[r] = term if step == 0 else raw[r] + term
+            for kh in range(3):
+                part = up_all[
+                    kw, :, kt * 8 : kt * 8 + 8, kh * in_channels : (kh + 1) * in_channels
+                ].astype(F32)
+                part = part.reshape(small, in_channels).astype(BF16)
+                for r in range(2):
+                    r_in = r + kh - 1
+                    if 0 <= r_in < 2:
+                        up_taps[
+                            kw, kt * pair + r * small : kt * pair + (r + 1) * small,
+                            r_in * in_channels : (r_in + 1) * in_channels,
+                        ] = part
+        term = lax.dot_general(
+            inputs[kw], up_taps[kw], (((1,), (1,)), ((), ())), preferred_element_type=F32
+        )
+        raw[...] = term if step == 0 else raw[...] + term
         if step == 0:
             ring_pass(1, 2)
 
     def frame(t):
         return slice(t * width, (t + 1) * width)
 
-    for r in range(2):
-        for t in range(times + 3):
-            if t % 2 == 0:
-                value = raw[r, frame(t // 2 + 1), 0:small] + raw[
-                    r, frame(t // 2), 2 * small : 3 * small
-                ]
-            else:
-                value = raw[r, frame((t + 1) // 2), small : 2 * small]
-            before[r, frame(t)] = value
-            active = value / (1.0 + jnp.exp(-value))
-            hidden[r, frame(t)] = active.astype(BF16).astype(F32)
-
-    for r in range(2):
-        @pl.loop(0, times)
-        def _(t):
-            parts = []
-            lines = [
-                hidden[r, pl.ds(pl.multiple_of((t + kt) * width, width), width)] for kt in range(3)
-            ]
-            for kw in range(3):
-                parts += [shifted(line, kw - 1) for line in lines]
-            at = pl.ds(pl.multiple_of(t * width, width), width)
-            for i, pair in enumerate(pairs(parts)):
-                patches[r, at, i * 2 * small : (i + 1) * 2 * small] = pair
+    for t in range(times + 3):
+        if t % 2 == 0:
+            value = raw[frame(t // 2 + 1), 0:pair] + raw[frame(t // 2), 2 * pair : 3 * pair]
+        else:
+            value = raw[frame((t + 1) // 2), pair : 2 * pair]
+        before[frame(t)] = value
+        active = (value / (1.0 + jnp.exp(-value))).astype(BF16)
+        for kw in range(3):
+            moved = shifted(active.astype(F32), kw - 1).astype(BF16)
+            for kt in range(3):
+                if 0 <= t - kt < times:
+                    patches[kw, frame(t - kt), kt * pair : (kt + 1) * pair] = moved
 
     def exchange(i, part, got):
         return [
@@ -437,29 +440,42 @@
         ]
 
     out_d = exchange(0, part_d, got_d)
-    for step, kh in enumerate(HEIGHTS):
-        ring_got(1, kh, 3)
-        for r in range(2):
-            r_in = r + kh - 1
-            if 0 <= r_in < 2:
-                term = lax.dot_general(
-                    patches[r_in], mix_all[kh], (((1,), (1,)), ((), ())),
-                    preferred_element_type=F32,
-                )
-                decoding[r] = term if step == 0 else decoding[r] + term
-        if step == 2:
+    lane = lax.broadcasted_iota(jnp.int32, (channels, pair), 1)
+    for step, kw in enumerate(TAPS_W):
+        ring_got(1, kw, 3)
+        last = mix_all[kw, :, 3 * pair : 4 * pair].astype(F32)
+        tails = [last, pltpu.roll(last, small, 1), mix_all[kw, :, 4 * pair : 5 * pair].astype(F32)]
+        for kt in range(3):
+            block = mix_all[kw, :, kt * pair : (kt + 1) * pair]
+            turned = pltpu.roll(block.astype(F32), small, 1)
+            mix_taps[kw, channels : 2 * channels, kt * pair : (kt + 1) * pair] = block
+            mix_taps[kw, 0:channels, kt * pair : (kt + 1) * pair] = jnp.where(
+                lane < small, turned, tails[kt]
+            ).astype(BF16)
+        term = lax.dot_general(
+            patches[kw], mix_taps[kw], (((1,), (1,)), ((), ())), preferred_element_type=F32
+        )
+        if step < 2:
+            decoding[...] = term if step == 0 else decoding[...] + term
+        else:
+            term = term + decoding[...]
             for r in range(2):
                 for t in range(times):
                     for c in range(4):
                         low = t * width + c * cols
-                        part_d[c, t, r] = decoding[r, low : low + cols].astype(BF16)
+                        part_d[c, t, r] = term[
+                            low : low + cols, r * channels : (r + 1) * channels
+                        ].astype(BF16)
             for copy in out_d:
                 copy.start()
-        for r in range(2):
-            r_in = r - kh + 1
-            if 0 <= r_in < 2:
-                term = jnp.dot(cots[r_in], mix_all[kh], preferred_element_type=F32)
-                spread[r] = term if step == 0 else spread[r] + term
+        spread[...] = jnp.dot(cots[...], mix_taps[kw], preferred_element_type=F32)
+        for t in range(times + 1):
+            part = None
+            for kt in range(3):
+                piece = spread[frame(t + 2 - kt), kt * pair : (kt + 1) * pair]
+                part = piece if part is None else part + piece
+            part = shifted(part, 1 - kw)
+            gradient[frame(t)] = part if step == 0 else gradient[frame(t)] + part
 
     def add_and_cross(i, part, got, summed, last, first_copies):
         for copy in first_copies:
@@ -475,42 +491,26 @@
 
     cross_d = add_and_cross(0, part_d, got_d, sum_d, last_d, out_d)
 
-    for r in range(2):
-        lines = []
-        for t in range(times + 1):
-            gradient = None
-            for kw in range(3):
-                part = None
-                for kt in range(3):
-                    low = (kw * 3 + kt) * small
-                    piece = spread[r, frame(t + 2 - kt), low : low + small]
-                    part = piece if part is None else part + piece
-                part = shifted(part, 1 - kw)
-                gradient = part if gradient is None else gradient + part
-            value = before[r, frame(t + 2)]
-            sigma = 1.0 / (1.0 + jnp.exp(-value))
-            gradient = gradient * sigma * (1.0 + value * (1.0 - sigma))
-            hidden[r, frame(t)] = gradient.astype(BF16).astype(F32)
-
-    for r in range(2):
-        for i in range(count):
-            lines = [hidden[r, frame(2 * i + kt)] for kt in range(3)]
-            for kw in range(3):
-                for j, pair in enumerate(pairs([shifted(line, 1 - kw) for line in lines])):
-                    grads[r, kw, frame(i), j * 2 * small : (j + 1) * 2 * small] = pair
+    for t in range(times + 1):
+        value = before[frame(t + 2)]
+        sigma = 1.0 / (1.0 + jnp.exp(-value))
+        line = gradient[frame(t)] * sigma * (1.0 + value * (1.0 - sigma))
+        line = line.astype(BF16).astype(F32)
+        for kw in range(3):
+            moved = shifted(line, 1 - kw).astype(BF16)
+            for kt in range(3):
+                if (t - kt) % 2 == 0 and 0 <= t - kt < 2 * count:
+                    grads[kw, frame((t - kt) // 2), kt * pair : (kt + 1) * pair] = moved
 
     out_g = []
     for r in range(2):
         total = None
-        for r_in in range(2):
-            kh = r - r_in + 1
-            for kw in range(3):
-                start = kw * in_channels
-                term = jnp.dot(
-                    grads[r_in, kw], up_taps[kh, :, start : start + in_channels],
-                    preferred_element_type=F32,
-                )
-                total = term if total is None else total + term
+        for kw in range(3):
+            term = jnp.dot(
+                grads[kw], up_taps[kw, :, r * in_channels : (r + 1) * in_channels],
+                preferred_element_type=F32,
+            )
+            total = term if total is None else total + term
         for i in range(count):
             for c in range(4):
                 low = i * width + c * cols
@@ -527,7 +527,17 @@
     ]
     for r in range(2):
         finish(part_g.at[r], got_g.at[r], last_g.at[r], cross_g[r], grad_ref.at[:, r])
-    for copy in list(copies.values()) + halos + own + crossing + beside + passed:
+
+    @pl.when(me < n - 1)
+    def _():
+        halos[0].wait_send()
+
+    @pl.when(me > 0)
+    def _():
+        halos[1].wait_send()
+        halos[2].wait_send()
+
+    for copy in list(copies.values()) + own + crossing + beside + passed:
         copy.wait_send()
     for copy in out_d + out_g[0] + out_g[1] + [cross_d] + cross_g:
         copy.wait_send()
@@ -556,16 +566,17 @@
             pltpu.VMEM((3, channels, 10 * small), BF16),
             pltpu.VMEM((4, count + 3, height, cols, in_channels), BF16),
             pltpu.VMEM((4, times + 3, height, cols, channels), BF16),
-            pltpu.VMEM((3, 4 * small, 3 * in_channels), BF16),
-            pltpu.VMEM((2, (count + 3) * width, 3 * in_channels), BF16),
-            pltpu.VMEM((2, (count + 3) * width, 4 * small), F32),
-            pltpu.VMEM((2, (times + 3) * width, small), F32),
-            pltpu.VMEM((2, (times + 3) * width, small), F32),
-            pltpu.VMEM((2, times * width, 10 * small), BF16),
-            pltpu.VMEM((2, times * width, channels), F32),
-            pltpu.VMEM((2, (times + 3) * width, channels), BF16),
-            pltpu.VMEM((2, (times + 3) * width, 10 * small), F32),
-            pltpu.VMEM((2, 3, count * width, 4 * small), BF16),
+            pltpu.VMEM((3, 6 * small, 2 * in_channels), BF16),
+            pltpu.VMEM((3, (count + 3) * width, 2 * in_channels), BF16),
+            pltpu.VMEM((3, 2 * channels, 6 * small), BF16),
+            pltpu.VMEM(((count + 3) * width, 6 * small), F32),
+            pltpu.VMEM(((times + 3) * width, 2 * small), F32),
+            pltpu.VMEM((3, times * width, 6 * small), BF16),
+            pltpu.VMEM((times * width, 2 * channels), F32),
+            pltpu.VMEM(((times + 3) * width, 2 * channels), BF16),
+            pltpu.VMEM(((times + 3) * width, 6 * small), F32),
+            pltpu.VMEM(((times + 1) * width, 2 * small), F32),
+            pltpu.VMEM((3, count * width, 6 * small), BF16),
             pltpu.VMEM((4,) + d_block, BF16),
             pltpu.VMEM((2, 4) + g_half, BF16),
             pltpu.VMEM((2,) + d_block, BF16),

time: 54.6 us -> 55.5 us (1.016)
  Pallas kernels: 51.6 us -> 52.4 us
    pallas_call x1, Pallas kernels: 51.6 us -> 52.4 us  [fused(): pl.pallas_call(functools.partial(fused_kernel, n), out_shape=(jax.ShapeDt...]
where the time goes in v4:
time: 55.5 us; the launch traced here: 55.3 us
  Pallas kernels  52.4 us (94%)
  local copies, waits for them, and re-layouts  2.26 us (4%)
  between operations  0.65 us (1%)
    pallas_call x1, Pallas kernels, fused(): pl.pallas_call(functools.partial(fused_kernel, n), out_shape=(jax.ShapeDt...  52.4 us
    unnamed x4, local copies, waits for them, and re-layouts  2.26 us

profile of v4, /device:TPU:0, one launch (start us, length us, event | category | flops | bytes accessed | tf_op | source)
XLA Modules:
  0.0 55.3 jit_solution(16920239451249559376)
XLA Ops:
  0.6 52.4 %shard_map.59 = (bf16[6,2,24,256]{3,2,1,0:T(8,128)(2,1)}, bf16[3,2,24,384]{3,2,1,0:T(8,128)(2,1)}) custom-call(bf16[32,10368]{1,0:T(8,128)(2,1)} %bitcast.2, bf16[32,6912]{1,0:T(8,128)(2,1)} %bitcast.3, bf16[3,2,24,384]{3,2,1,0:T(8,128)(2,1)} %frames_ref.1, bf16[6,2,24,256]{3,2,1,0:T(8,128)(2,1)} %cot_ref.1), custom_call_target="tpu_custom_call" | custom-call | tf_op jit(solution)/shard_map/pallas_call | solution.py:556
  53.0 0.0 copy-start
  53.0 1.6 %copy.8 = bf16[6,2,24,256]{3,2,1,0:T(8,128)(2,1)} copy(bf16[6,2,24,256]{3,2,1,0:T(8,128)(2,1)} %get-tuple-element.4) | data formatting | bytes 294912
  54.7 0.0 copy-done
  54.7 0.6 %copy.9 = bf16[3,2,24,384]{3,2,1,0:T(8,128)(2,1)} copy(bf16[3,2,24,384]{3,2,1,0:T(8,128)(2,1)S(1)} %copy-done) | data formatting | bytes 221184
Async XLA Ops:
  53.0 1.6 %copy-start = (bf16[3,2,24,384]{3,2,1,0:T(8,128)(2,1)S(1)}, bf16[3,2,24,384]{3,2,1,0:T(8,128)(2,1)}, u32[]{:S(2)}) copy-start(bf16[3,2,24,384]{3,2,1,0:T(8,128)(2,1)} %get-tuple-element.5) | copy-start | bytes 331780

commit v5 on v4

--- a/solution.py
+++ b/solution.py
@@ -243,7 +243,8 @@
         owner = ring_tm((place + (n - step if direction == 0 else step)) % n, n)
         target = right if direction == 0 else left
         ref = up_all.at[tap_w, owner] if kind == 0 else mix_all.at[
-            tap_w, pl.ds(pl.multiple_of(owner * rows, rows), rows)
+            tap_w, pl.ds(pl.multiple_of(owner * rows, rows), rows),
+            0 : (8 if tap_w == 0 else 10) * small,
         ]
         index = (direction, kind, tap_w, step)
         return remote(ref, ref, ring_send.at[index], ring_recv.at[index], target, q)
@@ -319,12 +320,13 @@
         return jnp.dot(jnp.concatenate(lines, axis=0), pick, preferred_element_type=F32)
 
     for kw in TAPS_W:
-        low = taken([(0, 0, kw), (1, 0, kw), (2, 0, kw), (1, 2, kw)], first)
-        high = taken([(0, 1, kw), (1, 1, kw), (2, 1, kw), (0, 2, kw), (2, 2, kw)], second)
-        for i in range(5):
-            part = high[i * rows : (i + 1) * rows]
-            if i < 4:
-                part = part + low[i * rows : (i + 1) * rows]
+        lows = [(0, 0, kw), (1, 0, kw), (2, 0, kw), (1, 2, kw)]
+        highs = [(0, 1, kw), (1, 1, kw), (2, 1, kw), (0, 2, kw)]
+        if kw > 0:
+            lows, highs = lows + [(2, 2, 0)], highs + [(2, 2, kw)]
+        low, high = taken(lows, first), taken(highs, second)
+        for i in range(len(lows)):
+            part = low[i * rows : (i + 1) * rows] + high[i * rows : (i + 1) * rows]
             mix_all[kw, mine, i * 2 * small : (i + 1) * 2 * small] = part.astype(BF16)
     ring_pass(0, 0)
     for tap_w in TAPS_W:
@@ -444,7 +446,10 @@
     for step, kw in enumerate(TAPS_W):
         ring_got(1, kw, 3)
         last = mix_all[kw, :, 3 * pair : 4 * pair].astype(F32)
-        tails = [last, pltpu.roll(last, small, 1), mix_all[kw, :, 4 * pair : 5 * pair].astype(F32)]
+        final = mix_all[max(kw, 1), :, 4 * pair : 5 * pair].astype(F32)
+        if kw == 0:
+            final = pltpu.roll(final, small, 1)
+        tails = [last, pltpu.roll(last, small, 1), final]
         for kt in range(3):
             block = mix_all[kw, :, kt * pair : (kt + 1) * pair]
             turned = pltpu.roll(block.astype(F32), small, 1)
@@ -489,8 +494,6 @@
         copy.wait_recv()
         out[...] = (part[q].astype(F32) + got[0].astype(F32) + last[...].astype(F32)).astype(BF16)
 
-    cross_d = add_and_cross(0, part_d, got_d, sum_d, last_d, out_d)
-
     for t in range(times + 1):
         value = before[frame(t + 2)]
         sigma = 1.0 / (1.0 + jnp.exp(-value))
@@ -501,6 +504,8 @@
             for kt in range(3):
                 if (t - kt) % 2 == 0 and 0 <= t - kt < 2 * count:
                     grads[kw, frame((t - kt) // 2), kt * pair : (kt + 1) * pair] = moved
+
+    cross_d = add_and_cross(0, part_d, got_d, sum_d, last_d, out_d)
 
     out_g = []
     for r in range(2):
@@ -543,6 +548,17 @@
         copy.wait_send()
 
 
+def place(made_d, made_g, decoded_ref, grad_ref, sems):
+    copies = [
+        pltpu.make_async_copy(made_d, decoded_ref, sems.at[0]),
+        pltpu.make_async_copy(made_g, grad_ref, sems.at[1]),
+    ]
+    for copy in copies:
+        copy.start()
+    for copy in copies:
+        copy.wait()
+
+
 def fused(frames, up_kernel, mix_kernel, cotangent):
     n = lax.axis_size("tm")
     count, height, cols, in_channels = frames.shape
@@ -553,7 +569,7 @@
     d_block, g_block = (times, height, cols, channels), (count, height, cols, in_channels)
     g_half = (count, cols, in_channels)
     dma = pltpu.SemaphoreType.DMA
-    return pl.pallas_call(
+    made = pl.pallas_call(
         functools.partial(fused_kernel, n),
         out_shape=(
             jax.ShapeDtypeStruct(d_block, BF16),
@@ -598,6 +614,14 @@
             collective_id=0, has_side_effects=True, vmem_limit_bytes=56 * 1024 * 1024
         ),
     )(up_rows, mix_rows, frames, cotangent)
+    anywhere = pl.BlockSpec(memory_space=pltpu.HBM)
+    return pl.pallas_call(
+        place,
+        out_shape=tuple(jax.ShapeDtypeStruct(array.shape, array.dtype) for array in made),
+        in_specs=[anywhere] * 2,
+        out_specs=(anywhere, anywhere),
+        scratch_shapes=[dma((2,))],
+    )(*made)
 
 
 def solution(mesh):

time: 55.5 us -> 61.7 us (1.11)
  Pallas kernels: 52.4 us -> 60.9 us
  local copies, waits for them, and re-layouts: 2.26 us -> 0 us
    pallas_call x0 -> x1, Pallas kernels: none -> 8.94 us  [fused(): pl.pallas_call(place, out_shape=tuple((jax.ShapeDtypeStruct(array.shape,...]
    unnamed x4 -> x0, local copies, waits for them, and re-layouts: 2.26 us -> none
where the time goes in v5:
time: 61.7 us; the launch traced here: 61.5 us
  Pallas kernels  60.9 us (99%)
  between operations  0.64 us (1%)
    pallas_call x1, Pallas kernels, fused(): pl.pallas_call(functools.partial(fused_kernel, n), out_shape=(jax.ShapeDt...  52 us
    pallas_call x1, Pallas kernels, fused(): pl.pallas_call(place, out_shape=tuple((jax.ShapeDtypeStruct(array.shape,...  8.94 us

profile of v5, /device:TPU:0, one launch (start us, length us, event | category | flops | bytes accessed | tf_op | source)
XLA Modules:
  0.0 61.5 jit_solution(11691549585664344194)
XLA Ops:
  0.6 52.0 %shard_map.59 = (bf16[6,2,24,256]{3,2,1,0:T(8,128)(2,1)}, bf16[3,2,24,384]{3,2,1,0:T(8,128)(2,1)}) custom-call(bf16[32,10368]{1,0:T(8,128)(2,1)} %bitcast.2, bf16[32,6912]{1,0:T(8,128)(2,1)} %bitcast.3, bf16[3,2,24,384]{3,2,1,0:T(8,128)(2,1)} %frames_ref.1, bf16[6,2,24,256]{3,2,1,0:T(8,128)(2,1)} %cot_ref.1), custom_call_target="tpu_custom_call" | custom-call | tf_op jit(solution)/shard_map/pallas_call | solution.py:572
  52.6 8.9 %shard_map.60 = (bf16[6,2,24,256]{3,2,1,0:T(8,128)(2,1)}, bf16[3,2,24,384]{3,2,1,0:T(8,128)(2,1)}) custom-call(bf16[6,2,24,256]{3,2,1,0:T(8,128)(2,1)} %get-tuple-element.4.made_d, bf16[3,2,24,384]{3,2,1,0:T(8,128)(2,1)} %get-tuple-element.5.made_g), custom_call_target="tpu_custom_call" | custom-call | tf_op jit(solution)/shard_map/pallas_call | solution.py:618

commit v6 on v5

--- a/solution.py
+++ b/solution.py
@@ -171,7 +171,6 @@
 MESH_ID = pl.DeviceIdType.MESH
 BF16 = jnp.bfloat16
 F32 = jnp.float32
-TAPS_W = (1, 0, 2)
 
 
 def shifted(rows, by):
@@ -193,7 +192,7 @@
 def fused_kernel(
     n, up_ref, mix_ref, frames_ref, cot_ref, decoded_ref, grad_ref,
     up_all, mix_all, frames_all, cot_all, up_taps, inputs, mix_taps, raw, before, patches, decoding,
-    cots, spread, gradient, grads, part_d, part_g, got_d, got_g, sum_d, sum_g, last_d, last_g,
+    cots, spread, gradient, grads, summed, part_d, part_g, got_d, got_g, sum_d, sum_g, last_d, last_g,
     ring_send, ring_recv, halo_send, halo_recv, col_send, col_recv, out_send, out_recv,
 ):
     me, q = lax.axis_index("tm"), lax.axis_index("col")
@@ -239,12 +238,12 @@
             ].astype(BF16)
     pl.semaphore_wait(barrier, 6)
 
-    def ring(direction, kind, tap_w, step):
+    def ring(direction, kind, tap_w, step, short):
         owner = ring_tm((place + (n - step if direction == 0 else step)) % n, n)
         target = right if direction == 0 else left
         ref = up_all.at[tap_w, owner] if kind == 0 else mix_all.at[
             tap_w, pl.ds(pl.multiple_of(owner * rows, rows), rows),
-            0 : (8 if tap_w == 0 else 10) * small,
+            0 : (8 if short else 10) * small,
         ]
         index = (direction, kind, tap_w, step)
         return remote(ref, ref, ring_send.at[index], ring_recv.at[index], target, q)
@@ -257,7 +256,7 @@
     def ring_start(kind, tap_w, step):
         for direction in range(2):
             if step < steps_of(direction, kind):
-                copy = ring(direction, kind, tap_w, step)
+                copy = ring(direction, kind, tap_w, step, tap_w == 1)
                 copies[direction, kind, tap_w, step] = copy
                 copy.start()
 
@@ -267,7 +266,7 @@
                 copies[direction, kind, tap_w, step].wait_recv()
 
     def ring_pass(kind, step):
-        for tap_w in TAPS_W:
+        for tap_w in range(3):
             ring_got(kind, tap_w, step)
             ring_start(kind, tap_w, step + 1)
 
@@ -298,7 +297,7 @@
         halos[1].start()
         halos[2].start()
 
-    for tap_w in TAPS_W:
+    for tap_w in range(3):
         ring_start(0, tap_w, 0)
     for copy in own:
         copy.start()
@@ -319,17 +318,17 @@
         ]
         return jnp.dot(jnp.concatenate(lines, axis=0), pick, preferred_element_type=F32)
 
-    for kw in TAPS_W:
+    for kw in range(3):
         lows = [(0, 0, kw), (1, 0, kw), (2, 0, kw), (1, 2, kw)]
         highs = [(0, 1, kw), (1, 1, kw), (2, 1, kw), (0, 2, kw)]
-        if kw > 0:
-            lows, highs = lows + [(2, 2, 0)], highs + [(2, 2, kw)]
+        if kw != 1:
+            lows, highs = lows + [(2, 2, 1)], highs + [(2, 2, kw)]
         low, high = taken(lows, first), taken(highs, second)
         for i in range(len(lows)):
             part = low[i * rows : (i + 1) * rows] + high[i * rows : (i + 1) * rows]
             mix_all[kw, mine, i * 2 * small : (i + 1) * 2 * small] = part.astype(BF16)
     ring_pass(0, 0)
-    for tap_w in TAPS_W:
+    for tap_w in range(3):
         ring_start(1, tap_w, 0)
 
     @pl.when(me > 0)
@@ -397,8 +396,17 @@
             cots[at, r * channels : (r + 1) * channels] = line.astype(BF16)
 
     pair = 2 * small
-    for step, kw in enumerate(TAPS_W):
+    for kw in range(3):
         ring_got(0, kw, 3)
+    ring_pass(1, 2)
+
+    def frame(t):
+        return pl.ds(pl.multiple_of(t * width, width), width)
+
+    raw[...] = jnp.zeros_like(raw)
+
+    @pl.loop(0, 3)
+    def _(kw):
         for kt in range(3):
             for kh in range(3):
                 part = up_all[
@@ -412,28 +420,25 @@
                             kw, kt * pair + r * small : kt * pair + (r + 1) * small,
                             r_in * in_channels : (r_in + 1) * in_channels,
                         ] = part
-        term = lax.dot_general(
+        raw[...] += lax.dot_general(
             inputs[kw], up_taps[kw], (((1,), (1,)), ((), ())), preferred_element_type=F32
         )
-        raw[...] = term if step == 0 else raw[...] + term
-        if step == 0:
-            ring_pass(1, 2)
-
-    def frame(t):
-        return slice(t * width, (t + 1) * width)
-
-    for t in range(times + 3):
-        if t % 2 == 0:
-            value = raw[frame(t // 2 + 1), 0:pair] + raw[frame(t // 2), 2 * pair : 3 * pair]
-        else:
-            value = raw[frame((t + 1) // 2), pair : 2 * pair]
+
+    def keep(t, value):
         before[frame(t)] = value
-        active = (value / (1.0 + jnp.exp(-value))).astype(BF16)
+        active = (value / (1.0 + jnp.exp(-value))).astype(BF16).astype(F32)
         for kw in range(3):
-            moved = shifted(active.astype(F32), kw - 1).astype(BF16)
+            moved = shifted(active, kw - 1).astype(BF16)
             for kt in range(3):
-                if 0 <= t - kt < times:
-                    patches[kw, frame(t - kt), kt * pair : (kt + 1) * pair] = moved
+                patches[kw, frame(t - kt + 2), kt * pair : (kt + 1) * pair] = moved
+
+    @pl.loop(0, count + 2)
+    def _(i):
+        keep(2 * i, raw[frame(i + 1), 0:pair] + raw[frame(i), 2 * pair : 3 * pair])
+
+    @pl.loop(0, count + 1)
+    def _(i):
+        keep(2 * i + 1, raw[frame(i + 1), pair : 2 * pair])
 
     def exchange(i, part, got):
         return [
@@ -443,50 +448,62 @@
 
     out_d = exchange(0, part_d, got_d)
     lane = lax.broadcasted_iota(jnp.int32, (channels, pair), 1)
-    for step, kw in enumerate(TAPS_W):
-        ring_got(1, kw, 3)
+    decoding[...] = jnp.zeros_like(decoding)
+    gradient[...] = jnp.zeros_like(gradient)
+
+    @pl.loop(0, 3)
+    def _(kw):
+        @pl.when(kw == 1)
+        def _():
+            ring(1, 1, kw, 3, True).wait_recv()
+
+        @pl.when(kw != 1)
+        def _():
+            ring(1, 1, kw, 3, False).wait_recv()
+
         last = mix_all[kw, :, 3 * pair : 4 * pair].astype(F32)
-        final = mix_all[max(kw, 1), :, 4 * pair : 5 * pair].astype(F32)
-        if kw == 0:
-            final = pltpu.roll(final, small, 1)
+        final = mix_all[kw - kw % 2, :, 4 * pair : 5 * pair].astype(F32)
+        final = jnp.where(kw == 1, pltpu.roll(final, small, 1), final)
         tails = [last, pltpu.roll(last, small, 1), final]
         for kt in range(3):
             block = mix_all[kw, :, kt * pair : (kt + 1) * pair]
             turned = pltpu.roll(block.astype(F32), small, 1)
-            mix_taps[kw, channels : 2 * channels, kt * pair : (kt + 1) * pair] = block
-            mix_taps[kw, 0:channels, kt * pair : (kt + 1) * pair] = jnp.where(
+            mix_taps[channels : 2 * channels, kt * pair : (kt + 1) * pair] = block
+            mix_taps[0:channels, kt * pair : (kt + 1) * pair] = jnp.where(
                 lane < small, turned, tails[kt]
             ).astype(BF16)
-        term = lax.dot_general(
-            patches[kw], mix_taps[kw], (((1,), (1,)), ((), ())), preferred_element_type=F32
+        decoding[...] += lax.dot_general(
+            patches[kw, 2 * width : (times + 2) * width], mix_taps[...],
+            (((1,), (1,)), ((), ())), preferred_element_type=F32,
         )
-        if step < 2:
-            decoding[...] = term if step == 0 else decoding[...] + term
-        else:
-            term = term + decoding[...]
-            for r in range(2):
-                for t in range(times):
-                    for c in range(4):
-                        low = t * width + c * cols
-                        part_d[c, t, r] = term[
-                            low : low + cols, r * channels : (r + 1) * channels
-                        ].astype(BF16)
-            for copy in out_d:
-                copy.start()
-        spread[...] = jnp.dot(cots[...], mix_taps[kw], preferred_element_type=F32)
-        for t in range(times + 1):
+        spread[...] = jnp.dot(cots[...], mix_taps[...], preferred_element_type=F32)
+
+        @pl.loop(0, times + 1)
+        def _(t):
             part = None
             for kt in range(3):
                 piece = spread[frame(t + 2 - kt), kt * pair : (kt + 1) * pair]
                 part = piece if part is None else part + piece
-            part = shifted(part, 1 - kw)
-            gradient[frame(t)] = part if step == 0 else gradient[frame(t)] + part
-
-    def add_and_cross(i, part, got, summed, last, first_copies):
+            part = jnp.where(
+                kw == 0, shifted(part, 1), jnp.where(kw == 1, part, shifted(part, -1))
+            )
+            gradient[frame(t)] += part
+
+    @pl.loop(0, times)
+    def _(t):
+        for r in range(2):
+            for c in range(4):
+                at = pl.ds(pl.multiple_of(t * width + c * cols, cols), cols)
+                part_d[c, t, r] = decoding[at, r * channels : (r + 1) * channels].astype(BF16)
+
+    for copy in out_d:
+        copy.start()
+
+    def add_and_cross(i, part, got, sums, last, first_copies):
         for copy in first_copies:
             copy.wait_recv()
-        summed[...] = (part[across].astype(F32) + got[1].astype(F32)).astype(BF16)
-        copy = remote(summed, last, out_send.at[i + 2], out_recv.at[i + 2], me, across)
+        sums[...] = (part[across].astype(F32) + got[1].astype(F32)).astype(BF16)
+        copy = remote(sums, last, out_send.at[i + 2], out_recv.at[i + 2], me, across)
         copy.start()
         return copy
 
@@ -494,32 +511,39 @@
         copy.wait_recv()
         out[...] = (part[q].astype(F32) + got[0].astype(F32) + last[...].astype(F32)).astype(BF16)
 
-    for t in range(times + 1):
+    @pl.loop(0, times + 1)
+    def _(t):
         value = before[frame(t + 2)]
         sigma = 1.0 / (1.0 + jnp.exp(-value))
         line = gradient[frame(t)] * sigma * (1.0 + value * (1.0 - sigma))
-        line = line.astype(BF16).astype(F32)
-        for kw in range(3):
-            moved = shifted(line, 1 - kw).astype(BF16)
-            for kt in range(3):
-                if (t - kt) % 2 == 0 and 0 <= t - kt < 2 * count:
-                    grads[kw, frame((t - kt) // 2), kt * pair : (kt + 1) * pair] = moved
+        gradient[frame(t)] = line.astype(BF16).astype(F32)
+
+    @pl.loop(0, count)
+    def _(i):
+        for kt in range(3):
+            line = gradient[frame(2 * i + kt)]
+            for kw in range(3):
+                grads[kw, frame(i), kt * pair : (kt + 1) * pair] = shifted(line, 1 - kw).astype(BF16)
 
     cross_d = add_and_cross(0, part_d, got_d, sum_d, last_d, out_d)
 
     out_g = []
     for r in range(2):
-        total = None
-        for kw in range(3):
-            term = jnp.dot(
+        summed[...] = jnp.zeros_like(summed)
+
+        @pl.loop(0, 3)
+        def _(kw):
+            summed[...] += jnp.dot(
                 grads[kw], up_taps[kw, :, r * in_channels : (r + 1) * in_channels],
                 preferred_element_type=F32,
             )
-            total = term if total is None else total + term
-        for i in range(count):
+
+        @pl.loop(0, count)
+        def _(i):
             for c in range(4):
-                low = i * width + c * cols
-                part_g[r, c, i] = total[low : low + cols].astype(BF16)
+                at = pl.ds(pl.multiple_of(i * width + c * cols, cols), cols)
+                part_g[r, c, i] = summed[at].astype(BF16)
+
         out_g.append(exchange(3 + 3 * r, part_g.at[r], got_g.at[r]))
         for copy in out_g[r]:
             copy.start()
@@ -548,15 +572,9 @@
         copy.wait_send()
 
 
-def place(made_d, made_g, decoded_ref, grad_ref, sems):
-    copies = [
-        pltpu.make_async_copy(made_d, decoded_ref, sems.at[0]),
-        pltpu.make_async_copy(made_g, grad_ref, sems.at[1]),
-    ]
-    for copy in copies:
-        copy.start()
-    for copy in copies:
-        copy.wait()
+def place(made_d, made_g, decoded_ref, grad_ref):
+    decoded_ref[...] = made_d[...]
+    grad_ref[...] = made_g[...]
 
 
 def fused(frames, up_kernel, mix_kernel, cotangent):
@@ -584,15 +602,16 @@
             pltpu.VMEM((4, times + 3, height, cols, channels), BF16),
             pltpu.VMEM((3, 6 * small, 2 * in_channels), BF16),
             pltpu.VMEM((3, (count + 3) * width, 2 * in_channels), BF16),
-            pltpu.VMEM((3, 2 * channels, 6 * small), BF16),
+            pltpu.VMEM((2 * channels, 6 * small), BF16),
             pltpu.VMEM(((count + 3) * width, 6 * small), F32),
             pltpu.VMEM(((times + 3) * width, 2 * small), F32),
-            pltpu.VMEM((3, times * width, 6 * small), BF16),
+            pltpu.VMEM((3, (times + 5) * width, 6 * small), BF16),
             pltpu.VMEM((times * width, 2 * channels), F32),
             pltpu.VMEM(((times + 3) * width, 2 * channels), BF16),
             pltpu.VMEM(((times + 3) * width, 6 * small), F32),
             pltpu.VMEM(((times + 1) * width, 2 * small), F32),
             pltpu.VMEM((3, count * width, 6 * small), BF16),
+            pltpu.VMEM((count * width, in_channels), F32),
             pltpu.VMEM((4,) + d_block, BF16),
             pltpu.VMEM((2, 4) + g_half, BF16),
             pltpu.VMEM((2,) + d_block, BF16),
@@ -614,13 +633,11 @@
             collective_id=0, has_side_effects=True, vmem_limit_bytes=56 * 1024 * 1024
         ),
     )(up_rows, mix_rows, frames, cotangent)
-    anywhere = pl.BlockSpec(memory_space=pltpu.HBM)
     return pl.pallas_call(
         place,
         out_shape=tuple(jax.ShapeDtypeStruct(array.shape, array.dtype) for array in made),
-        in_specs=[anywhere] * 2,
-        out_specs=(anywhere, anywhere),
-        scratch_shapes=[dma((2,))],
+        in_specs=[whole] * 2,
+        out_specs=(whole, whole),
     )(*made)
 
 

time: 61.7 us -> 53.4 us (0.87)
  Pallas kernels: 60.9 us -> 52.6 us
    pallas_call x1, Pallas kernels: 8.94 us -> 1.68 us  [fused(): pl.pallas_call(place, out_shape=tuple((jax.ShapeDtypeStruct(array.shape,...]
    pallas_call x1, Pallas kernels: 52 us -> 50.9 us  [fused(): pl.pallas_call(functools.partial(fused_kernel, n), out_shape=(jax.ShapeDt...]
where the time goes in v6:
time: 53.4 us; the launch traced here: 53.2 us
  Pallas kernels  52.6 us (99%)
  between operations  0.64 us (1%)
    pallas_call x1, Pallas kernels, fused(): pl.pallas_call(functools.partial(fused_kernel, n), out_shape=(jax.ShapeDt...  50.9 us
    pallas_call x1, Pallas kernels, fused(): pl.pallas_call(place, out_shape=tuple((jax.ShapeDtypeStruct(array.shape,...  1.68 us

profile of v6, /device:TPU:0, one launch (start us, length us, event | category | flops | bytes accessed | tf_op | source)
XLA Modules:
  0.0 53.2 jit_solution(13346927258930910549)
XLA Ops:
  0.6 50.9 %shard_map.59 = (bf16[6,2,24,256]{3,2,1,0:T(8,128)(2,1)}, bf16[3,2,24,384]{3,2,1,0:T(8,128)(2,1)}) custom-call(bf16[32,10368]{1,0:T(8,128)(2,1)} %bitcast.2, bf16[32,6912]{1,0:T(8,128)(2,1)} %bitcast.3, bf16[3,2,24,384]{3,2,1,0:T(8,128)(2,1)} %frames_ref.1, bf16[6,2,24,256]{3,2,1,0:T(8,128)(2,1)} %cot_ref.1), custom_call_target="tpu_custom_call" | custom-call | tf_op jit(solution)/shard_map/pallas_call | solution.py:590
  51.6 1.7 %shard_map.60 = (bf16[6,2,24,256]{3,2,1,0:T(8,128)(2,1)}, bf16[3,2,24,384]{3,2,1,0:T(8,128)(2,1)}) custom-call(bf16[6,2,24,256]{3,2,1,0:T(8,128)(2,1)} %get-tuple-element.4.made_d, bf16[3,2,24,384]{3,2,1,0:T(8,128)(2,1)} %get-tuple-element.5.made_g), custom_call_target="tpu_custom_call" | custom-call | tf_op jit(solution)/shard_map/pallas_call | solution.py:636

commit v7 on v6

--- a/solution.py
+++ b/solution.py
@@ -238,25 +238,25 @@
             ].astype(BF16)
     pl.semaphore_wait(barrier, 6)
 
-    def ring(direction, kind, tap_w, step, short):
+    def ring(direction, kind, tap_w, step):
         owner = ring_tm((place + (n - step if direction == 0 else step)) % n, n)
         target = right if direction == 0 else left
         ref = up_all.at[tap_w, owner] if kind == 0 else mix_all.at[
             tap_w, pl.ds(pl.multiple_of(owner * rows, rows), rows),
-            0 : (8 if short else 10) * small,
+            0 : (8 if tap_w == 1 else 10) * small,
         ]
         index = (direction, kind, tap_w, step)
         return remote(ref, ref, ring_send.at[index], ring_recv.at[index], target, q)
 
     def steps_of(direction, kind):
-        return n // 2 if direction == kind else n // 2 - 1
+        return n // 2 if direction != kind else n // 2 - 1
 
     copies = {}
 
     def ring_start(kind, tap_w, step):
         for direction in range(2):
             if step < steps_of(direction, kind):
-                copy = ring(direction, kind, tap_w, step, tap_w == 1)
+                copy = ring(direction, kind, tap_w, step)
                 copies[direction, kind, tap_w, step] = copy
                 copy.start()
 
@@ -448,57 +448,6 @@
 
     out_d = exchange(0, part_d, got_d)
     lane = lax.broadcasted_iota(jnp.int32, (channels, pair), 1)
-    decoding[...] = jnp.zeros_like(decoding)
-    gradient[...] = jnp.zeros_like(gradient)
-
-    @pl.loop(0, 3)
-    def _(kw):
-        @pl.when(kw == 1)
-        def _():
-            ring(1, 1, kw, 3, True).wait_recv()
-
-        @pl.when(kw != 1)
-        def _():
-            ring(1, 1, kw, 3, False).wait_recv()
-
-        last = mix_all[kw, :, 3 * pair : 4 * pair].astype(F32)
-        final = mix_all[kw - kw % 2, :, 4 * pair : 5 * pair].astype(F32)
-        final = jnp.where(kw == 1, pltpu.roll(final, small, 1), final)
-        tails = [last, pltpu.roll(last, small, 1), final]
-        for kt in range(3):
-            block = mix_all[kw, :, kt * pair : (kt + 1) * pair]
-            turned = pltpu.roll(block.astype(F32), small, 1)
-            mix_taps[channels : 2 * channels, kt * pair : (kt + 1) * pair] = block
-            mix_taps[0:channels, kt * pair : (kt + 1) * pair] = jnp.where(
-                lane < small, turned, tails[kt]
-            ).astype(BF16)
-        decoding[...] += lax.dot_general(
-            patches[kw, 2 * width : (times + 2) * width], mix_taps[...],
-            (((1,), (1,)), ((), ())), preferred_element_type=F32,
-        )
-        spread[...] = jnp.dot(cots[...], mix_taps[...], preferred_element_type=F32)
-
-        @pl.loop(0, times + 1)
-        def _(t):
-            part = None
-            for kt in range(3):
-                piece = spread[frame(t + 2 - kt), kt * pair : (kt + 1) * pair]
-                part = piece if part is None else part + piece
-            part = jnp.where(
-                kw == 0, shifted(part, 1), jnp.where(kw == 1, part, shifted(part, -1))
-            )
-            gradient[frame(t)] += part
-
-    @pl.loop(0, times)
-    def _(t):
-        for r in range(2):
-            for c in range(4):
-                at = pl.ds(pl.multiple_of(t * width + c * cols, cols), cols)
-                part_d[c, t, r] = decoding[at, r * channels : (r + 1) * channels].astype(BF16)
-
-    for copy in out_d:
-        copy.start()
-
     def add_and_cross(i, part, got, sums, last, first_copies):
         for copy in first_copies:
             copy.wait_recv()
@@ -511,6 +460,56 @@
         copy.wait_recv()
         out[...] = (part[q].astype(F32) + got[0].astype(F32) + last[...].astype(F32)).astype(BF16)
 
+    def decode(kw):
+        ring_got(1, kw, 3)
+        last = mix_all[kw, :, 3 * pair : 4 * pair].astype(F32)
+        final = mix_all[kw - kw % 2, :, 4 * pair : 5 * pair].astype(F32)
+        if kw == 1:
+            final = pltpu.roll(final, small, 1)
+        tails = [last, pltpu.roll(last, small, 1), final]
+        for kt in range(3):
+            block = mix_all[kw, :, kt * pair : (kt + 1) * pair]
+            turned = pltpu.roll(block.astype(F32), small, 1)
+            mix_taps[kw, channels : 2 * channels, kt * pair : (kt + 1) * pair] = block
+            mix_taps[kw, 0:channels, kt * pair : (kt + 1) * pair] = jnp.where(
+                lane < small, turned, tails[kt]
+            ).astype(BF16)
+        term = lax.dot_general(
+            patches[kw, 2 * width : (times + 2) * width], mix_taps[kw],
+            (((1,), (1,)), ((), ())), preferred_element_type=F32,
+        )
+        decoding[...] = term if kw == 0 else decoding[...] + term
+
+    def back(kw):
+        spread[...] = jnp.dot(cots[...], mix_taps[kw], preferred_element_type=F32)
+
+        @pl.loop(0, times + 1)
+        def _(t):
+            part = None
+            for kt in range(3):
+                piece = spread[frame(t + 2 - kt), kt * pair : (kt + 1) * pair]
+                part = piece if part is None else part + piece
+            part = shifted(part, 1 - kw)
+            gradient[frame(t)] = part if kw == 0 else gradient[frame(t)] + part
+
+    decode(0)
+    back(0)
+    decode(1)
+    decode(2)
+
+    @pl.loop(0, times)
+    def _(t):
+        for r in range(2):
+            for c in range(4):
+                at = pl.ds(pl.multiple_of(t * width + c * cols, cols), cols)
+                part_d[c, t, r] = decoding[at, r * channels : (r + 1) * channels].astype(BF16)
+
+    for copy in out_d:
+        copy.start()
+    back(1)
+    cross_d = add_and_cross(0, part_d, got_d, sum_d, last_d, out_d)
+    back(2)
+
     @pl.loop(0, times + 1)
     def _(t):
         value = before[frame(t + 2)]
@@ -524,8 +523,6 @@
             line = gradient[frame(2 * i + kt)]
             for kw in range(3):
                 grads[kw, frame(i), kt * pair : (kt + 1) * pair] = shifted(line, 1 - kw).astype(BF16)
-
-    cross_d = add_and_cross(0, part_d, got_d, sum_d, last_d, out_d)
 
     out_g = []
     for r in range(2):
@@ -602,7 +599,7 @@
             pltpu.VMEM((4, times + 3, height, cols, channels), BF16),
             pltpu.VMEM((3, 6 * small, 2 * in_channels), BF16),
             pltpu.VMEM((3, (count + 3) * width, 2 * in_channels), BF16),
-            pltpu.VMEM((2 * channels, 6 * small), BF16),
+            pltpu.VMEM((3, 2 * channels, 6 * small), BF16),
             pltpu.VMEM(((count + 3) * width, 6 * small), F32),
             pltpu.VMEM(((times + 3) * width, 2 * small), F32),
             pltpu.VMEM((3, (times + 5) * width, 6 * small), BF16),

time: 53.4 us -> 52.5 us (0.983)
  Pallas kernels: 52.6 us -> 51.7 us
    pallas_call x1, Pallas kernels: 50.9 us -> 50.1 us  [fused(): pl.pallas_call(functools.partial(fused_kernel, n), out_shape=(jax.ShapeDt...]
where the time goes in v7:
time: 52.5 us; the launch traced here: 52.4 us
  Pallas kernels  51.7 us (98%)
  between operations  0.64 us (1%)
    pallas_call x1, Pallas kernels, fused(): pl.pallas_call(functools.partial(fused_kernel, n), out_shape=(jax.ShapeDt...  50.1 us
    pallas_call x1, Pallas kernels, fused(): pl.pallas_call(place, out_shape=tuple((jax.ShapeDtypeStruct(array.shape,...  1.68 us

profile of v7, /device:TPU:0, one launch (start us, length us, event | category | flops | bytes accessed | tf_op | source)
XLA Modules:
  0.0 52.4 jit_solution(9387476231062779320)
XLA Ops:
  0.6 50.1 %shard_map.59 = (bf16[6,2,24,256]{3,2,1,0:T(8,128)(2,1)}, bf16[3,2,24,384]{3,2,1,0:T(8,128)(2,1)}) custom-call(bf16[32,10368]{1,0:T(8,128)(2,1)} %bitcast.2, bf16[32,6912]{1,0:T(8,128)(2,1)} %bitcast.3, bf16[3,2,24,384]{3,2,1,0:T(8,128)(2,1)} %frames_ref.1, bf16[6,2,24,256]{3,2,1,0:T(8,128)(2,1)} %cot_ref.1), custom_call_target="tpu_custom_call" | custom-call | tf_op jit(solution)/shard_map/pallas_call | solution.py:587
  50.7 1.7 %shard_map.60 = (bf16[6,2,24,256]{3,2,1,0:T(8,128)(2,1)}, bf16[3,2,24,384]{3,2,1,0:T(8,128)(2,1)}) custom-call(bf16[6,2,24,256]{3,2,1,0:T(8,128)(2,1)} %get-tuple-element.4.made_d, bf16[3,2,24,384]{3,2,1,0:T(8,128)(2,1)} %get-tuple-element.5.made_g), custom_call_target="tpu_custom_call" | custom-call | tf_op jit(solution)/shard_map/pallas_call | solution.py:633

commit v8 on v7

--- a/solution.py
+++ b/solution.py
@@ -253,22 +253,23 @@
 
     copies = {}
 
-    def ring_start(kind, tap_w, step):
-        for direction in range(2):
+    def ring_start(kind, tap_w, step, directions=(0, 1)):
+        for direction in directions:
             if step < steps_of(direction, kind):
                 copy = ring(direction, kind, tap_w, step)
                 copies[direction, kind, tap_w, step] = copy
                 copy.start()
 
-    def ring_got(kind, tap_w, step):
-        for direction in range(2):
+    def ring_got(kind, tap_w, step, directions=(0, 1)):
+        for direction in directions:
             if step < steps_of(direction, kind):
                 copies[direction, kind, tap_w, step].wait_recv()
 
     def ring_pass(kind, step):
         for tap_w in range(3):
-            ring_got(kind, tap_w, step)
-            ring_start(kind, tap_w, step + 1)
+            for direction in range(2):
+                ring_got(kind, tap_w, step, (direction,))
+                ring_start(kind, tap_w, step + 1, (direction,))
 
     own = [
         remote(src, dst, col_send.at[i], col_recv.at[i], me, col)
@@ -544,13 +545,13 @@
         out_g.append(exchange(3 + 3 * r, part_g.at[r], got_g.at[r]))
         for copy in out_g[r]:
             copy.start()
-    finish(part_d, got_d, last_d, cross_d, decoded_ref)
     cross_g = [
         add_and_cross(
             3 + 3 * r, part_g.at[r], got_g.at[r], sum_g.at[r], last_g.at[r], out_g[r]
         )
         for r in range(2)
     ]
+    finish(part_d, got_d, last_d, cross_d, decoded_ref)
     for r in range(2):
         finish(part_g.at[r], got_g.at[r], last_g.at[r], cross_g[r], grad_ref.at[:, r])
 

time: 52.5 us -> 50.4 us (0.960)
  Pallas kernels: 51.7 us -> 49.6 us
    pallas_call x1, Pallas kernels: 50.1 us -> 47.9 us  [fused(): pl.pallas_call(functools.partial(fused_kernel, n), out_shape=(jax.ShapeDt...]
where the time goes in v8:
time: 50.4 us; the launch traced here: 50.3 us
  Pallas kernels  49.6 us (98%)
  between operations  0.64 us (1%)
    pallas_call x1, Pallas kernels, fused(): pl.pallas_call(functools.partial(fused_kernel, n), out_shape=(jax.ShapeDt...  47.9 us
    pallas_call x1, Pallas kernels, fused(): pl.pallas_call(place, out_shape=tuple((jax.ShapeDtypeStruct(array.shape,...  1.68 us

profile of v8, /device:TPU:0, one launch (start us, length us, event | category | flops | bytes accessed | tf_op | source)
XLA Modules:
  0.0 50.3 jit_solution(16580532520727108452)
XLA Ops:
  0.6 47.9 %shard_map.59 = (bf16[6,2,24,256]{3,2,1,0:T(8,128)(2,1)}, bf16[3,2,24,384]{3,2,1,0:T(8,128)(2,1)}) custom-call(bf16[32,10368]{1,0:T(8,128)(2,1)} %bitcast.2, bf16[32,6912]{1,0:T(8,128)(2,1)} %bitcast.3, bf16[3,2,24,384]{3,2,1,0:T(8,128)(2,1)} %frames_ref.1, bf16[6,2,24,256]{3,2,1,0:T(8,128)(2,1)} %cot_ref.1), custom_call_target="tpu_custom_call" | custom-call | tf_op jit(solution)/shard_map/pallas_call | solution.py:588
  48.6 1.7 %shard_map.60 = (bf16[6,2,24,256]{3,2,1,0:T(8,128)(2,1)}, bf16[3,2,24,384]{3,2,1,0:T(8,128)(2,1)}) custom-call(bf16[6,2,24,256]{3,2,1,0:T(8,128)(2,1)} %get-tuple-element.4.made_d, bf16[3,2,24,384]{3,2,1,0:T(8,128)(2,1)} %get-tuple-element.5.made_g), custom_call_target="tpu_custom_call" | custom-call | tf_op jit(solution)/shard_map/pallas_call | solution.py:634

commit v9 on v8

--- a/solution.py
+++ b/solution.py
@@ -265,9 +265,9 @@
             if step < steps_of(direction, kind):
                 copies[direction, kind, tap_w, step].wait_recv()
 
-    def ring_pass(kind, step):
+    def ring_pass(kind, step, directions=(0, 1)):
         for tap_w in range(3):
-            for direction in range(2):
+            for direction in directions:
                 ring_got(kind, tap_w, step, (direction,))
                 ring_start(kind, tap_w, step + 1, (direction,))
 
@@ -367,6 +367,7 @@
     ring_pass(0, 1)
     ring_pass(1, 0)
     ring_pass(0, 2)
+    ring_pass(1, 1)
     for copy in own[:2] + crossing:
         copy.wait_recv()
     passed = [
@@ -375,7 +376,6 @@
     ]
     for copy in passed:
         copy.start()
-    ring_pass(1, 1)
     for copy in own[2:] + beside + passed:
         copy.wait_recv()
 
@@ -397,9 +397,9 @@
             cots[at, r * channels : (r + 1) * channels] = line.astype(BF16)
 
     pair = 2 * small
+    ring_pass(1, 2, (0,))
     for kw in range(3):
         ring_got(0, kw, 3)
-    ring_pass(1, 2)
 
     def frame(t):
         return pl.ds(pl.multiple_of(t * width, width), width)
@@ -462,6 +462,7 @@
         out[...] = (part[q].astype(F32) + got[0].astype(F32) + last[...].astype(F32)).astype(BF16)
 
     def decode(kw):
+        ring_got(1, kw, 2, (1,))
         ring_got(1, kw, 3)
         last = mix_all[kw, :, 3 * pair : 4 * pair].astype(F32)
         final = mix_all[kw - kw % 2, :, 4 * pair : 5 * pair].astype(F32)

time: 50.4 us -> 48.3 us (0.958)
  Pallas kernels: 49.6 us -> 47.5 us
    pallas_call x1, Pallas kernels: 47.9 us -> 45.8 us  [fused(): pl.pallas_call(functools.partial(fused_kernel, n), out_shape=(jax.ShapeDt...]
where the time goes in v9:
time: 48.3 us; the launch traced here: 48.1 us
  Pallas kernels  47.5 us (98%)
  between operations  0.64 us (1%)
    pallas_call x1, Pallas kernels, fused(): pl.pallas_call(functools.partial(fused_kernel, n), out_shape=(jax.ShapeDt...  45.8 us
    pallas_call x1, Pallas kernels, fused(): pl.pallas_call(place, out_shape=tuple((jax.ShapeDtypeStruct(array.shape,...  1.68 us

profile of v9, /device:TPU:0, one launch (start us, length us, event | category | flops | bytes accessed | tf_op | source)
XLA Modules:
  0.0 48.1 jit_solution(8691789825150134706)
XLA Ops:
  0.6 45.8 %shard_map.59 = (bf16[6,2,24,256]{3,2,1,0:T(8,128)(2,1)}, bf16[3,2,24,384]{3,2,1,0:T(8,128)(2,1)}) custom-call(bf16[32,10368]{1,0:T(8,128)(2,1)} %bitcast.2, bf16[32,6912]{1,0:T(8,128)(2,1)} %bitcast.3, bf16[3,2,24,384]{3,2,1,0:T(8,128)(2,1)} %frames_ref.1, bf16[6,2,24,256]{3,2,1,0:T(8,128)(2,1)} %cot_ref.1), custom_call_target="tpu_custom_call" | custom-call | tf_op jit(solution)/shard_map/pallas_call | solution.py:589
  46.4 1.7 %shard_map.60 = (bf16[6,2,24,256]{3,2,1,0:T(8,128)(2,1)}, bf16[3,2,24,384]{3,2,1,0:T(8,128)(2,1)}) custom-call(bf16[6,2,24,256]{3,2,1,0:T(8,128)(2,1)} %get-tuple-element.4.made_d, bf16[3,2,24,384]{3,2,1,0:T(8,128)(2,1)} %get-tuple-element.5.made_g), custom_call_target="tpu_custom_call" | custom-call | tf_op jit(solution)/shard_map/pallas_call | solution.py:635
